TPU v7x, 512 devices: a whole 4x8x8 slice. The times are simulated.
512 devices in a mesh: mode: 32 (over y, x_hi, core), wave: 16 (over x_lo, z).
Axes of the slice: x: 4 (x_hi: 2, x_lo: 2; x = x_hi * 2 + x_lo), y: 8, z: 8, core: 2. Of those that a mesh axis runs over, the one named last changes fastest.
Arguments:
- field_in: bfloat16 [16, 32, 2, 512, 512], P('wave', 'mode'), may hold values from -6 to 6
- target: bfloat16 [16, 32, 2, 512, 512], P('wave', 'mode'), may hold values from -6 to 6
- mask_old: bfloat16 [2, 512, 512], replicated, may hold values from -1 to 1
- scales: float32 [16], P('wave'), may hold values from 0.5 to 2
Outputs:
- mask_one: bfloat16 [2, 512, 512], P(None, 'mode')
- mask_two: bfloat16 [2, 512, 512], P(None, 'mode')
All inputs are finite; a program needn't handle non-finite values.
Results may differ from a plain program's by a relative error of at most 0.013.
Values may be sent and summed in bfloat16 or wider, within the bound.
No kernel may reach another device: no remote copies, remote signals or barrier semaphores. Data moves between devices by JAX's collectives and lax.ppermute only.
A program may use at most 64 MiB of HBM per device.

v0:
```python
import jax
import jax.numpy as jnp
from jax import lax
from jax.sharding import PartitionSpec as P


def chirp(scale, count):
    pos = jnp.arange(count, dtype=jnp.float32)
    diff = pos[:, None] - pos[None, :]
    angle = jnp.pi * scale * diff * diff / count
    factor = jnp.float32(count) ** (-0.5)
    return (
        (jnp.cos(angle) * factor).astype(jnp.bfloat16),
        (jnp.sin(angle) * factor).astype(jnp.bfloat16),
    )


def right_matrix(real_part, imag_part, sign):
    upper = jnp.concatenate([real_part, sign * imag_part], 1)
    lower = jnp.concatenate([-sign * imag_part, real_part], 1)
    return jnp.concatenate([upper, lower], 0)


def left_matrix(real_part, imag_part, sign):
    first = jnp.concatenate([real_part, sign * imag_part], 0)
    second = jnp.concatenate([-sign * imag_part, real_part], 0)
    return jnp.stack([first, second], 0)


def right_product(field_re, field_im, right):
    joined = jnp.concatenate([field_re, field_im], -1)
    return jnp.einsum("brk,kc->brc", joined, right, preferred_element_type=jnp.float32).astype(
        jnp.bfloat16
    )


def left_product(middle, left):
    batch = middle.shape[0]
    count = middle.shape[1]
    shaped = middle.reshape(batch, count, 2, count)
    result = jnp.einsum("pqk,bkpc->bqc", left, shaped, preferred_element_type=jnp.float32)
    return (result[:, :count], result[:, count:])


def phasor_rows(total, power_sum, count):
    power = power_sum / (count * count)
    real_part = total[:, :count]
    imag_part = total[:, count:]
    factor = lax.rsqrt(real_part * real_part + imag_part * imag_part + power + 1e-06)
    return jnp.concatenate([real_part * factor, imag_part * factor], -1).astype(jnp.bfloat16)


def as_output(mask_part, count):
    return jnp.stack([mask_part[:, :count], mask_part[:, count:]], 0)


def whole_mask(term):
    total = lax.psum(term, ("mode", "wave"))
    return phasor_rows(total, jnp.sum(total * total), term.shape[1] // 2)


def local(field_in, target, mask_old, scales):
    count = field_in.shape[-1]
    row_count = count // lax.axis_size("mode")
    kernel_re, kernel_im = chirp(scales[0], count)
    f_re = field_in[0, :, 0]
    f_im = field_in[0, :, 1]
    b_re = target[0, :, 0].astype(jnp.float32)
    b_im = target[0, :, 1].astype(jnp.float32)
    old_re = mask_old[0].astype(jnp.float32)
    old_im = mask_old[1].astype(jnp.float32)
    c_re = (b_re * old_re + b_im * old_im).astype(jnp.bfloat16)
    c_im = (b_im * old_re - b_re * old_im).astype(jnp.bfloat16)
    middle = right_product(c_re, c_im, right_matrix(kernel_re, kernel_im, -1.0))
    back_re, back_im = left_product(middle, left_matrix(kernel_re, kernel_im, -1.0))
    fr32 = f_re.astype(jnp.float32)
    fi32 = f_im.astype(jnp.float32)
    term_one = jnp.concatenate(
        [jnp.sum(back_re * fr32 + back_im * fi32, 0), jnp.sum(back_im * fr32 - back_re * fi32, 0)],
        -1,
    )
    forward_right = right_matrix(kernel_re, kernel_im, 1.0)
    mask_full = whole_mask(term_one)
    new_re = mask_full[:, :count].astype(jnp.float32)
    new_im = mask_full[:, count:].astype(jnp.float32)
    g_re = (fr32 * new_re - fi32 * new_im).astype(jnp.bfloat16)
    g_im = (fr32 * new_im + fi32 * new_re).astype(jnp.bfloat16)
    ahead_mid = right_product(g_re, g_im, forward_right)
    first_rows = lax.dynamic_slice_in_dim(
        mask_full, lax.axis_index("mode") * row_count, row_count, 0
    )
    ahead_re, ahead_im = left_product(ahead_mid, left_matrix(kernel_re, kernel_im, 1.0))
    term_two = jnp.concatenate(
        [
            jnp.sum(b_re * ahead_re + b_im * ahead_im, 0),
            jnp.sum(b_im * ahead_re - b_re * ahead_im, 0),
        ],
        -1,
    )
    second_full = whole_mask(term_two)
    second_rows = lax.dynamic_slice_in_dim(
        second_full, lax.axis_index("mode") * row_count, row_count, 0
    )
    return (as_output(first_rows, count), as_output(second_rows, count))


def solution(mesh):
    in_specs = (
        P("wave", "mode", None, None, None),
        P("wave", "mode", None, None, None),
        P(),
        P("wave"),
    )
    out_specs = (P(None, "mode", None), P(None, "mode", None))
    return jax.shard_map(local, mesh=mesh, in_specs=in_specs, out_specs=out_specs, check_vma=False)
```

profile of v0, /device:TPU:1, one launch (start us, length us, event | category | flops | bytes accessed | tf_op | source)
XLA Modules:
  0.0 623.1 jit_solution(12935222703062530760)
XLA Ops:
  7.9 3.8 broadcast_multiply_fusion
  11.8 4.4 multiply_convert_fusion.4
  16.2 4.4 multiply_convert_fusion.5
  20.6 0.2 copy.30
  21.1 1.5 fusion.72
  23.0 3.7 fusion.41
  26.7 0.4 fusion.52
  27.1 0.6 copy-done.12
  27.9 1.3 fusion.27
  29.2 1.3 copy.28
  31.0 0.8 copy-done.18
  31.8 2.8 fusion.21
  34.6 0.4 fusion.47
  35.0 1.5 pad_maximum_fusion.6
  36.6 0.2 all-reduce.5.cloned.1.call-start
  36.8 284.8 %all-reduce.3.cloned.1.call-done = f32[512,1024]{0,1:T(8,128)} async-done(((f32[512,1024]{0,1:T(8,128)}), f32[512,1024]{0,1:T(8,128)}) %all-reduce.3.cloned.1.call-update) | async-done | bytes 2097168 | tf_op jit(solution)/shard_map/psum | solution.py:58
  321.7 2.9 multiply_reduce_fusion.1
  325.2 0.5 fusion.64
  325.8 0.3 fusion.63
  326.1 0.5 copy-done.2
  326.7 0.4 copy-done.11
  327.5 1.3 fusion.24
  328.8 0.5 copy.29
  329.3 0.7 copy-done.19
  330.0 2.6 fusion.18
  332.6 0.4 fusion.56
  333.0 1.5 pad_maximum_fusion.7
  334.5 275.9 %all-reduce.5.cloned.1.call-done = f32[512,1024]{0,1:T(8,128)} async-done(((f32[512,1024]{0,1:T(8,128)}), f32[512,1024]{0,1:T(8,128)}) %all-reduce.5.cloned.1.call-update) | async-done | bytes 2097168 | tf_op jit(solution)/shard_map/psum | solution.py:58
  610.4 2.9 multiply_reduce_fusion
  614.0 0.3 multiply_convert_fusion
  615.1 0.6 pad_maximum_fusion.13
  615.7 0.6 pad_maximum_fusion.12
  (52 shorter events, 2.7 us)
Async XLA Ops:
  7.2 13.4 %copy-start.16 = (bf16[1,1,2,512,512]{4,3,2,1,0:T(8,128)(2,1)S(1)}, bf16[1,1,2,512,512]{4,3,2,1,0:T(8,128)(2,1)}, u32[]{:S(2)}) copy-start(bf16[1,1,2,512,512]{4,3,2,1,0:T(8,128)(2,1)} %param.5) | copy-start | bytes 3145732
  7.2 314.5 %all-reduce.3.cloned.1.call-start = ((), (), s32[]{:S(2)}) async-start(), calls=%async_computation | async-start | bytes 4194304 | tf_op jit(solution)/shard_map/psum | solution.py:58
  11.7 15.4 %copy-start.10 = (bf16[512,512]{1,0:T(8,128)(2,1)}, bf16[512,512]{1,0:T(8,128)(2,1)S(1)}, u32[]{:S(2)}) copy-start(bf16[512,512]{1,0:T(8,128)(2,1)S(1)} %broadcast_multiply_fusion) | copy-start | bytes 1572868
  20.8 5.9 copy-start.6
  21.0 5.6 copy-start.8
  26.7 1.0 copy-start.12
  26.7 1.2 copy-start.14
  29.2 1.3 copy-start.17
  30.6 1.2 copy-start.18
  36.6 573.8 %all-reduce.5.cloned.1.call-start = ((), (), s32[]{:S(2)}) async-start(), calls=%async_computation.1 | async-start | bytes 4194304 | tf_op jit(solution)/shard_map/psum | solution.py:58
  321.7 3.5 copy-start
  325.7 0.8 copy-start.2
  325.7 1.0 copy-start.4
  325.8 1.4 copy-start.11
  325.8 1.6 copy-start.13
  325.8 1.7 copy-start.15
  328.8 1.2 copy-start.19
  330.0 2.6 copy-start.7
  330.0 2.6 copy-start.9
  610.3 3.6 copy-start.1
  613.2 1.1 copy-start.3
  613.2 1.2 copy-start.5
Sparse Core Ops, SparseCore 0:
  36.7 284.9 all-reduce.2
  334.6 275.6 all-reduce.4
where the time goes:
time: 624 us; the launch traced here: 623 us
  waiting for transfers between devices  561 us (90%)
  other arithmetic  28.8 us (5%)
  between operations  16.5 us (3%)
  local copies, waits for them, and re-layouts  8.96 us (1%)
  matrix products  7.94 us (1%)
    psum x2, waiting for transfers between devices, whole_mask(): total = lax.psum(term, ('mode', 'wave'))  561 us
  transfers between devices with their start and end apart: 2, of which 2 were waited for; matrix products, arithmetic and copies ran while one was open for 0% of the time, Pallas kernels for 0%

commit v1 on v0

v1 whole, which is shorter than its diff:
```python
import jax
import jax.numpy as jnp
from jax import lax
from jax.experimental import pallas as pl
from jax.experimental.pallas import tpu as pltpu
from jax.sharding import Mesh, PartitionSpec as P

N = 512
BF = jnp.bfloat16
F32 = jnp.float32
AXES = ("y", "xh", "c", "xl", "z")
SIZES = (8, 2, 2, 2, 8)
MODE = ("y", "xh", "c")
WAVE = ("xl", "z")
VMEM_LIMIT = 40 * 1024 * 1024
BLK = 128


def dot(a, b):
    return jnp.dot(a, b, preferred_element_type=F32)


def chirp_into(scale, ar, ai):
    lane = lax.broadcasted_iota(jnp.int32, (8, 2 * N), 1)
    diff = (lane - N).astype(F32)
    angle = jnp.float32(jnp.pi) * scale * diff * diff / N
    factor = jnp.float32(N) ** (-0.5)
    for ref, fn in ((ar, jnp.cos), (ai, jnp.sin)):
        line = fn(angle) * factor
        for d in range(-3, 4):
            start = N + BLK * d - BLK
            window = line[0:1, start : start + 2 * BLK]
            window = jnp.broadcast_to(window, (BLK, 2 * BLK))
            rolled = pltpu.roll(window, BLK, 1, stride=1, stride_axis=0)
            block = rolled[:, :BLK].astype(BF)
            for row in range(4):
                col = row + d
                if 0 <= col < 4:
                    ref[row * BLK : (row + 1) * BLK, col * BLK : (col + 1) * BLK] = block


def back_kernel(scale_ref, core_ref, tgt_hbm, old_hbm, fld_hbm, ar, ai, keep, send, tgt, old, fld, z_s, sems):
    copies = [
        pltpu.make_async_copy(src, dst, sems.at[i])
        for i, (src, dst) in enumerate(((tgt_hbm, tgt), (old_hbm, old), (fld_hbm, fld)))
    ]
    for copy in copies:
        copy.start()
    chirp_into(scale_ref[0], ar, ai)
    copies[0].wait()
    copies[1].wait()
    for r in range(0, N, BLK):
        rows = slice(r, r + BLK)
        br = tgt[0, rows].astype(F32)
        bi = tgt[1, rows].astype(F32)
        mr = old[0, rows].astype(F32)
        mi = old[1, rows].astype(F32)
        cr = (br * mr + bi * mi).astype(BF)
        ci = (bi * mr - br * mi).astype(BF)
        z_s[0, rows] = (dot(cr, ar[...]) + dot(ci, ai[...])).astype(BF)
        z_s[1, rows] = (dot(ci, ar[...]) - dot(cr, ai[...])).astype(BF)
    copies[2].wait()
    first = core_ref[0] == 0
    for r in range(0, N, BLK):
        rows = slice(r, r + BLK)
        kr = ar[rows]
        ki = ai[rows]
        back_r = dot(kr, z_s[0]) + dot(ki, z_s[1])
        back_i = dot(kr, z_s[1]) - dot(ki, z_s[0])
        fr = fld[0, rows].astype(F32)
        fi = fld[1, rows].astype(F32)
        term_r = back_r * fr + back_i * fi
        term_i = back_i * fr - back_r * fi
        keep[rows] = jnp.where(first, term_r, term_i)
        send[rows] = jnp.where(first, term_i, term_r).astype(BF)


def ahead_kernel(core_ref, mode_ref, own, other, ar, ai, tgt_hbm, fld_hbm, mask_out, keep, send, tgt, fld, mask, z_s, sems):
    copies = [
        pltpu.make_async_copy(src, dst, sems.at[i])
        for i, (src, dst) in enumerate(((fld_hbm, fld), (tgt_hbm, tgt)))
    ]
    for copy in copies:
        copy.start()
    first = core_ref[0] == 0
    total = jnp.zeros((8, N), F32)
    for r in range(0, N, 8):
        a = own[r // 8].astype(F32)
        b = other[r // 8].astype(F32)
        total = total + (a * a + b * b)
    bias = jnp.sum(total) / (N * N) + 1e-06
    copies[0].wait()
    for r in range(0, N, BLK):
        rows = slice(r, r + BLK)
        a = own[r // 8 : (r + BLK) // 8].reshape(BLK, N).astype(F32)
        b = other[r // 8 : (r + BLK) // 8].reshape(BLK, N).astype(F32)
        factor = lax.rsqrt(a * a + b * b + bias)
        a = a * factor
        b = b * factor
        mr = jnp.where(first, a, b).astype(BF)
        mi = jnp.where(first, b, a).astype(BF)
        mask[0, rows] = mr
        mask[1, rows] = mi
        mr = mr.astype(F32)
        mi = mi.astype(F32)
        fr = fld[0, rows].astype(F32)
        fi = fld[1, rows].astype(F32)
        gr = (fr * mr - fi * mi).astype(BF)
        gi = (fr * mi + fi * mr).astype(BF)
        z_s[0, rows] = (dot(gr, ar[...]) - dot(gi, ai[...])).astype(BF)
        z_s[1, rows] = (dot(gi, ar[...]) + dot(gr, ai[...])).astype(BF)
    start = pl.multiple_of(mode_ref[0] * 16, 16)
    mask_out[0] = mask[0, pl.ds(start, 16)]
    mask_out[1] = mask[1, pl.ds(start, 16)]
    copies[1].wait()
    for r in range(0, N, BLK):
        rows = slice(r, r + BLK)
        kr = ar[rows]
        ki = ai[rows]
        ahead_r = dot(kr, z_s[0]) - dot(ki, z_s[1])
        ahead_i = dot(kr, z_s[1]) + dot(ki, z_s[0])
        br = tgt[0, rows].astype(F32)
        bi = tgt[1, rows].astype(F32)
        term_r = br * ahead_r + bi * ahead_i
        term_i = bi * ahead_r - br * ahead_i
        for q in range(BLK // 32):
            for part, term in ((0, term_r), (1, term_i)):
                even = term[q * 32 : q * 32 + 16]
                odd = term[q * 32 + 16 : q * 32 + 32]
                keep[r // 32 + q, part] = jnp.where(first, even, odd)
                send[r // 32 + q, part] = jnp.where(first, odd, even).astype(BF)


ANY = pl.BlockSpec(memory_space=pl.ANY)
SMEM = pl.BlockSpec(memory_space=pltpu.SMEM)
VMEM = pl.BlockSpec(memory_space=pltpu.VMEM)
PARAMS = pltpu.CompilerParams(vmem_limit_bytes=VMEM_LIMIT)


def call_back(scale, core, tgt, old, fld):
    return pl.pallas_call(
        back_kernel,
        out_shape=(
            jax.ShapeDtypeStruct((N, N), BF),
            jax.ShapeDtypeStruct((N, N), BF),
            jax.ShapeDtypeStruct((N, N), F32),
            jax.ShapeDtypeStruct((N, N), BF),
        ),
        in_specs=[SMEM, SMEM, ANY, ANY, ANY],
        out_specs=(VMEM,) * 4,
        scratch_shapes=[
            pltpu.VMEM((2, N, N), BF),
            pltpu.VMEM((2, N, N), BF),
            pltpu.VMEM((2, N, N), BF),
            pltpu.VMEM((2, N, N), BF),
            pltpu.SemaphoreType.DMA((3,)),
        ],
        compiler_params=PARAMS,
        name="back_margin",
    )(scale, core, tgt, old, fld)


def call_ahead(core, mode, own, other, ar, ai, tgt, fld):
    return pl.pallas_call(
        ahead_kernel,
        out_shape=(
            jax.ShapeDtypeStruct((2, 16, N), BF),
            jax.ShapeDtypeStruct((16, 2, 16, N), F32),
            jax.ShapeDtypeStruct((16, 2, 16, N), BF),
        ),
        in_specs=[SMEM, SMEM, VMEM, VMEM, VMEM, VMEM, ANY, ANY],
        out_specs=(VMEM,) * 3,
        scratch_shapes=[
            pltpu.VMEM((2, N, N), BF),
            pltpu.VMEM((2, N, N), BF),
            pltpu.VMEM((2, N, N), BF),
            pltpu.VMEM((2, N, N), BF),
            pltpu.SemaphoreType.DMA((2,)),
        ],
        compiler_params=PARAMS,
        name="ahead_margin",
    )(core, mode, own, other, ar, ai, tgt, fld)


def exchange(x, axes):
    return lax.all_to_all(x, axes, 0, 0, tiled=True)


def spread(x, axes, count):
    return exchange(jnp.broadcast_to(x[None], (count,) + x.shape), axes)


def total_of(x):
    return jnp.sum(x.astype(F32), 0)


def swap_cores(x):
    return lax.ppermute(x, "c", [(0, 1), (1, 0)])


def local(field_in, target, mask_old, scales):
    fld = field_in[0, 0]
    tgt = target[0, 0]
    core = lax.axis_index("c").reshape(1)
    mode = lax.axis_index(MODE).reshape(1)
    ar, ai, keep, send = call_back(scales, core, tgt, mask_old, fld)
    half = (keep + swap_cores(send).astype(F32)).astype(BF)
    part = total_of(exchange(half.reshape(64, 8, N), ("y", "z"))).astype(BF)
    part = total_of(spread(part, ("xh", "xl"), 4)).astype(BF)
    own = spread(part, ("y", "z"), 64)
    other = swap_cores(own)
    mask_one, keep, send = call_ahead(core, mode, own, other, ar, ai, tgt, fld)
    half = (keep + swap_cores(send).astype(F32)).astype(BF)
    part = total_of(exchange(half, ("y", "xh"))).astype(BF)
    rows = total_of(spread(part, WAVE, 16))
    power = jnp.sum(rows * rows)
    power = spread(jnp.broadcast_to(power.reshape(1, 1), (1, 128)), MODE, 32)
    power = jnp.sum(power[:, :, :1]) / (N * N)
    factor = lax.rsqrt(rows[0] * rows[0] + rows[1] * rows[1] + power + 1e-06)
    return mask_one, (rows * factor[None]).astype(BF)


def solution(mesh):
    fine = Mesh(mesh.devices.reshape(SIZES), AXES)
    data = P(WAVE, MODE, None, None, None)
    rows = P(None, MODE, None)
    return jax.shard_map(
        local,
        mesh=fine,
        in_specs=(data, data, P(), P(WAVE)),
        out_specs=(rows, rows),
        check_vma=False,
    )
```

time: 624 us -> 156 us (0.25)
  waiting for transfers between devices: 561 us -> 4.67 us
  blocking collectives: 0 us -> 113 us
  other arithmetic: 28.8 us -> 2.53 us
  starting transfers between devices: 0.26 us -> 18.3 us
  between operations: 16.5 us -> 2.07 us
  Pallas kernels: 0 us -> 8.98 us
  matrix products: 7.94 us -> 0 us
    psum x2 -> x0, waiting for transfers between devices: 561 us -> none  [whole_mask(): total = lax.psum(term, ('mode', 'wave'))]
    all_to_all x0 -> x6, blocking collectives: none -> 113 us  [exchange(): return lax.all_to_all(x, axes, 0, 0, tiled=True)]
    ppermute x0 -> x3, starting transfers between devices: none -> 18.3 us  [swap_cores(): return lax.ppermute(x, 'c', [(0, 1), (1, 0)])]
    convert_element_type x5 -> x2, other arithmetic: 9.96 us -> 0.83 us  [the longest x1 0.62 us: local(): return (mask_one, (rows * factor[None]).astype(BF))]
    pallas_call x0 -> x2, Pallas kernels: none -> 8.98 us  [the longest x1 5.41 us: call_ahead(): pl.pallas_call(ahead_kernel, out_shape=(jax.ShapeDtypeStruct((2, 16, N),...]
    dot_general x4 -> x0, matrix products: 7.94 us -> none  [the longest x2 5.42 us: left_product(): jnp.einsum('pqk,bkpc->bqc', left, shaped, preferred_element_type=jnp.floa...]
  transfers between devices with their start and end apart: 2 -> 3, of which waited for: 2 -> 3; matrix products, arithmetic and copies ran while one was open for 0% -> 0% of each run, Pallas kernels for 0% -> 0%
where the time goes in v1:
time: 156 us; the launch traced here: 155 us
  blocking collectives  113 us (72%)
  starting transfers between devices  18.3 us (12%)
  Pallas kernels  8.98 us (6%)
  local copies, waits for them, and re-layouts  5.47 us (4%)
  waiting for transfers between devices  4.67 us (3%)
  other arithmetic  2.53 us (2%)
  between operations  2.07 us (1%)
    all_to_all x6, blocking collectives, exchange(): return lax.all_to_all(x, axes, 0, 0, tiled=True)  113 us
    ppermute x3, starting transfers between devices, swap_cores(): return lax.ppermute(x, 'c', [(0, 1), (1, 0)])  18.3 us
    pallas_call x1, Pallas kernels, call_ahead(): pl.pallas_call(ahead_kernel, out_shape=(jax.ShapeDtypeStruct((2, 16, N),...  5.41 us
    unnamed x14, local copies, waits for them, and re-layouts  4.72 us
    ppermute x3, waiting for transfers between devices, swap_cores(): return lax.ppermute(x, 'c', [(0, 1), (1, 0)])  4.67 us
    pallas_call x1, Pallas kernels, call_back(): pl.pallas_call(back_kernel, out_shape=(jax.ShapeDtypeStruct((N, N), BF),...  3.57 us
  transfers between devices with their start and end apart: 3, of which 3 were waited for; matrix products, arithmetic and copies ran while one was open for 0% of the time, Pallas kernels for 0%

profile of v1, /device:TPU:1, one launch (start us, length us, event | category | flops | bytes accessed | tf_op | source)
XLA Modules:
  0.0 155.0 jit_solution(7546162486712958240)
XLA Ops:
  1.3 0.0 copy-start
  1.3 1.2 copy-done
  2.5 1.2 copy-done.2
  3.7 1.2 copy-done.4
  5.0 3.6 %back_margin.1 = (bf16[512,512]{1,0:T(8,128)(2,1)S(1)}, bf16[512,512]{1,0:T(8,128)(2,1)S(1)}, f32[512,512]{1,0:T(8,128)S(1)}, bf16[512,512]{1,0:T(8,128)(2,1)S(1)}) custom-call(f32[1]{0:T(128)S(6)} %copy.8.scale_ref, s32[1]{0:T(128)} %bitcast.core_ref, bf16[2,512,512]{2,1,0:T(8,128)(2,1)S(1)} %bitcast.8, bf16[2,512,512]{2,1,0:T(8,128)(2,1)S(1)} %copy-done.4, ...), custom_call_target="tpu_custom_call" | custom-call | tf_op jit(solution)/shard_map/back_margin/pallas_call | solution.py:141
  8.5 0.0 copy-start.5
  8.5 8.8 %collective-permute-start = (bf16[512,512]{1,0:T(8,128)(2,1)S(1)}, bf16[512,512]{1,0:T(8,128)(2,1)S(1)}, u32[]{:S(2)}, u32[]{:S(2)}) collective-permute-start(bf16[512,512]{1,0:T(8,128)(2,1)S(1)} %get-tuple-element.10), channel_id=1, source_target_pairs={{0,16},{16,0},{1,17},{17,1},{2,18},{18,2},{3,19},{19,3},{4,20},{20... | collective-permute-start | bytes 1572872 | tf_op jit(solution)/shard_map/ppermute | solution.py:198
  17.3 1.5 collective-permute-done
  18.9 0.2 fusion
  19.0 0.0 copy-done.5
  19.0 27.4 %all_to_all.30 = bf16[64,8,512]{2,1,0:T(8,128)(2,1)S(1)} all-to-all(bf16[64,8,512]{2,1,0:T(8,128)(2,1)S(1)} %fusion), channel_id=1, replica_groups=mesh['y'=8,'xh'=2,'c'=2,'xl'=2,'z'=8] {'y','z'}, dimensions={0} | all-to-all | bytes 1048576 | tf_op jit(solution)/shard_map/all_to_all | solution.py:186
  46.5 0.1 reduce_sum.63
  46.6 8.2 %all_to_all.31 = bf16[4,8,512]{2,1,0:T(8,128)(2,1)S(1)} all-to-all(bf16[4,8,512]{2,1,0:T(8,128)(2,1)S(1)} %broadcast_in_dim.6), channel_id=1, replica_groups=mesh['y'=8,'xh'=2,'c'=2,'xl'=2,'z'=8] {'xh','xl'}, dimensions={0} | all-to-all | bytes 65536 | tf_op jit(solution)/shard_map/all_to_all | solution.py:186
  54.9 22.6 %all_to_all.32.own = bf16[64,8,512]{2,1,0:T(8,128)(2,1)S(1)} all-to-all(bf16[64,8,512]{2,1,0:T(8,128)(2,1)S(1)} %broadcast_in_dim.7), channel_id=1, replica_groups=mesh['y'=8,'xh'=2,'c'=2,'xl'=2,'z'=8] {'y','z'}, dimensions={0} | all-to-all | bytes 1048576 | tf_op jit(solution)/shard_map/all_to_all | solution.py:186
  77.5 7.2 %collective-permute-start.1 = (bf16[64,8,512]{2,1,0:T(8,128)(2,1)S(1)}, bf16[64,8,512]{2,1,0:T(8,128)(2,1)}, u32[]{:S(2)}, u32[]{:S(2)}) collective-permute-start(bf16[64,8,512]{2,1,0:T(8,128)(2,1)S(1)} %all_to_all.32.own), channel_id=1, source_target_pairs={{0,16},{16,0},{1,17},{17,1},{2,18},{18,2},{3,19},{19,3},{4,20},{20... | collective-permute-start | bytes 1572872 | tf_op jit(solution)/shard_map/ppermute | solution.py:198
  84.7 1.6 %collective-permute-done.1.other = bf16[64,8,512]{2,1,0:T(8,128)(2,1)} collective-permute-done((bf16[64,8,512]{2,1,0:T(8,128)(2,1)S(1)}, bf16[64,8,512]{2,1,0:T(8,128)(2,1)}, u32[]{:S(2)}, u32[]{:S(2)}) %collective-permute-start.1) | collective-permute-done | bytes 524320 | tf_op jit(solution)/shard_map/ppermute | solution.py:198
  86.4 0.0 copy-done.1
  86.4 1.0 copy-done.6
  87.4 5.4 %ahead_margin.1 = (bf16[2,16,512]{2,1,0:T(8,128)(2,1)}, f32[16,2,16,512]{3,2,1,0:T(8,128)S(1)}, bf16[16,2,16,512]{3,2,1,0:T(8,128)(2,1)S(1)}) custom-call(s32[1]{0:T(128)} %bitcast.core_ref, s32[1]{0:T(128)} %bitcast.1.mode_ref, bf16[64,8,512]{2,1,0:T(8,128)(2,1)S(1)} %all_to_all.32.own, bf16[64,8,512]{2,1,0:T(8,128)(2,1)} %collective-permute-done.1.other, ...), custom_call_target="tpu_custom_call" | custom-call | tf_op jit(solution)/shard_map/ahead_margin/pallas_call | solution.py:164
  92.8 2.3 %collective-permute-start.2 = (bf16[16,2,16,512]{3,2,1,0:T(8,128)(2,1)S(1)}, bf16[16,2,16,512]{3,2,1,0:T(8,128)(2,1)S(1)}, u32[]{:S(2)}, u32[]{:S(2)}) collective-permute-start(bf16[16,2,16,512]{3,2,1,0:T(8,128)(2,1)S(1)} %get-tuple-element.15), channel_id=1, source_target_pairs={{0,16},{16,0},{1,17},{17,1},{2,18},{18,2},{3,19},{19,3},{4,20},{20... | collective-permute-start | bytes 1572872 | tf_op jit(solution)/shard_map/ppermute | solution.py:198
  95.1 1.5 collective-permute-done.2
  96.7 0.2 add_convert_fusion
  96.9 21.8 %all_to_all.33 = bf16[16,2,16,512]{3,2,1,0:T(8,128)(2,1)S(1)} all-to-all(bf16[16,2,16,512]{3,2,1,0:T(8,128)(2,1)S(1)} %add_convert_fusion), channel_id=1, replica_groups=mesh['y'=8,'xh'=2,'c'=2,'xl'=2,'z'=8] {'y','xh'}, dimensions={0} | all-to-all | bytes 1048576 | tf_op jit(solution)/shard_map/all_to_all | solution.py:186
  118.6 0.1 reduce_sum.65
  118.7 0.1 broadcast_in_dim.8
  118.8 15.0 %all_to_all.34 = bf16[16,2,16,512]{3,2,1,0:T(8,128)(2,1)S(1)} all-to-all(bf16[16,2,16,512]{3,2,1,0:T(8,128)(2,1)S(1)} %broadcast_in_dim.8), channel_id=1, replica_groups=mesh['y'=8,'xh'=2,'c'=2,'xl'=2,'z'=8] {'xl','z'}, dimensions={0} | all-to-all | bytes 1048576 | tf_op jit(solution)/shard_map/all_to_all | solution.py:186
  133.8 0.1 convert_reduce_fusion
  133.9 0.6 multiply_reduce_fusion
  134.5 0.7 broadcast_in_dim_broadcast_in_dim_broadcast_in_dim.2
  135.1 17.9 %all_to_all.35 = f32[32,1,128]{2,1,0:T(1,128)S(1)} all-to-all(f32[32,1,128]{2,1,0:T(1,128)S(1)} %broadcast_in_dim_broadcast_in_dim_broadcast_in_dim.2), channel_id=1, replica_groups=mesh['y'=8,'xh'=2,'c'=2,'xl'=2,'z'=8] {'y','xh','c'}, dimensions={0} | all-to-all | bytes 32768 | tf_op jit(solution)/shard_map/all_to_all | solution.py:186
  153.0 0.6 slice_reduce_fusion
  154.4 0.6 multiply_convert_fusion
  (10 shorter events, 0.1 us)
Async XLA Ops:
  1.3 1.2 copy-start
  2.5 1.2 copy-start.2
  3.7 1.2 copy-start.4
  8.5 10.5 %copy-start.5 = (bf16[512,512]{1,0:T(8,128)(2,1)}, bf16[512,512]{1,0:T(8,128)(2,1)S(1)}, u32[]{:S(2)}) copy-start(bf16[512,512]{1,0:T(8,128)(2,1)S(1)} %get-tuple-element.12.ai) | copy-start | bytes 1572868
  8.5 10.3 %collective-permute-start = (bf16[512,512]{1,0:T(8,128)(2,1)S(1)}, bf16[512,512]{1,0:T(8,128)(2,1)S(1)}, u32[]{:S(2)}, u32[]{:S(2)}) collective-permute-start(bf16[512,512]{1,0:T(8,128)(2,1)S(1)} %get-tuple-element.10), channel_id=1, source_target_pairs={{0,16},{16,0},{1,17},{17,1},{2,18},{18,2},{3,19},{19,3},{4,20},{20... | collective-permute-start | bytes 1572872 | tf_op jit(solution)/shard_map/ppermute | solution.py:198
  46.5 39.9 %copy-start.1 = (bf16[1,1,2,512,512]{4,3,2,1,0:T(8,128)(2,1)S(1)}, bf16[1,1,2,512,512]{4,3,2,1,0:T(8,128)(2,1)}, u32[]{:S(2)}) copy-start(bf16[1,1,2,512,512]{4,3,2,1,0:T(8,128)(2,1)} %param.5) | copy-start | bytes 3145732
  46.5 39.9 %copy-start.3 = (bf16[1,1,2,512,512]{4,3,2,1,0:T(8,128)(2,1)S(1)}, bf16[1,1,2,512,512]{4,3,2,1,0:T(8,128)(2,1)}, u32[]{:S(2)}) copy-start(bf16[1,1,2,512,512]{4,3,2,1,0:T(8,128)(2,1)} %param.4) | copy-start | bytes 3145732
  77.5 8.9 %collective-permute-start.1 = (bf16[64,8,512]{2,1,0:T(8,128)(2,1)S(1)}, bf16[64,8,512]{2,1,0:T(8,128)(2,1)}, u32[]{:S(2)}, u32[]{:S(2)}) collective-permute-start(bf16[64,8,512]{2,1,0:T(8,128)(2,1)S(1)} %all_to_all.32.own), channel_id=1, source_target_pairs={{0,16},{16,0},{1,17},{17,1},{2,18},{18,2},{3,19},{19,3},{4,20},{20... | collective-permute-start | bytes 1572872 | tf_op jit(solution)/shard_map/ppermute | solution.py:198
  86.4 1.0 copy-start.6
  92.8 3.8 %collective-permute-start.2 = (bf16[16,2,16,512]{3,2,1,0:T(8,128)(2,1)S(1)}, bf16[16,2,16,512]{3,2,1,0:T(8,128)(2,1)S(1)}, u32[]{:S(2)}, u32[]{:S(2)}) collective-permute-start(bf16[16,2,16,512]{3,2,1,0:T(8,128)(2,1)S(1)} %get-tuple-element.15), channel_id=1, source_target_pairs={{0,16},{16,0},{1,17},{17,1},{2,18},{18,2},{3,19},{19,3},{4,20},{20... | collective-permute-start | bytes 1572872 | tf_op jit(solution)/shard_map/ppermute | solution.py:198

commit v2 on v1

--- a/solution.py
+++ b/solution.py
@@ -12,7 +12,7 @@
 SIZES = (8, 2, 2, 2, 8)
 MODE = ("y", "xh", "c")
 WAVE = ("xl", "z")
-VMEM_LIMIT = 40 * 1024 * 1024
+MIB = 1024 * 1024
 BLK = 128
 
 
@@ -75,25 +75,18 @@
         send[rows] = jnp.where(first, term_i, term_r).astype(BF)
 
 
-def ahead_kernel(core_ref, mode_ref, own, other, ar, ai, tgt_hbm, fld_hbm, mask_out, keep, send, tgt, fld, mask, z_s, sems):
-    copies = [
-        pltpu.make_async_copy(src, dst, sems.at[i])
-        for i, (src, dst) in enumerate(((fld_hbm, fld), (tgt_hbm, tgt)))
-    ]
-    for copy in copies:
-        copy.start()
+def ahead_kernel(core_ref, mode_ref, own, other, ar, ai, tgt, fld, mask_out, keep, send, mask, z_s):
     first = core_ref[0] == 0
-    total = jnp.zeros((8, N), F32)
-    for r in range(0, N, 8):
-        a = own[r // 8].astype(F32)
-        b = other[r // 8].astype(F32)
+    total = jnp.zeros((32, N), F32)
+    for r in range(16):
+        a = own[r].astype(F32)
+        b = other[r].astype(F32)
         total = total + (a * a + b * b)
     bias = jnp.sum(total) / (N * N) + 1e-06
-    copies[0].wait()
-    for r in range(0, N, BLK):
-        rows = slice(r, r + BLK)
-        a = own[r // 8 : (r + BLK) // 8].reshape(BLK, N).astype(F32)
-        b = other[r // 8 : (r + BLK) // 8].reshape(BLK, N).astype(F32)
+    for r in range(0, N, BLK):
+        rows = slice(r, r + BLK)
+        a = own[r // 32 : (r + BLK) // 32].reshape(BLK, N).astype(F32)
+        b = other[r // 32 : (r + BLK) // 32].reshape(BLK, N).astype(F32)
         factor = lax.rsqrt(a * a + b * b + bias)
         a = a * factor
         b = b * factor
@@ -112,7 +105,6 @@
     start = pl.multiple_of(mode_ref[0] * 16, 16)
     mask_out[0] = mask[0, pl.ds(start, 16)]
     mask_out[1] = mask[1, pl.ds(start, 16)]
-    copies[1].wait()
     for r in range(0, N, BLK):
         rows = slice(r, r + BLK)
         kr = ar[rows]
@@ -131,10 +123,29 @@
                 send[r // 32 + q, part] = jnp.where(first, odd, even).astype(BF)
 
 
-ANY = pl.BlockSpec(memory_space=pl.ANY)
+def power_kernel(parts, rows, power):
+    total = parts[0].astype(F32)
+    for w in range(1, 16):
+        total = total + parts[w].astype(F32)
+    rows[...] = total
+    power[...] = jnp.broadcast_to(jnp.sum(total * total), (32, 1, 128))
+
+
+def phasor_kernel(rows, power, out):
+    total = power[0]
+    for w in range(1, 32):
+        total = total + power[w]
+    bias = total[:, :1] / (N * N) + 1e-06
+    a = rows[0]
+    b = rows[1]
+    factor = lax.rsqrt(a * a + b * b + bias)
+    out[0] = (a * factor).astype(BF)
+    out[1] = (b * factor).astype(BF)
+
+
+HBM = pl.BlockSpec(memory_space=pltpu.HBM)
 SMEM = pl.BlockSpec(memory_space=pltpu.SMEM)
 VMEM = pl.BlockSpec(memory_space=pltpu.VMEM)
-PARAMS = pltpu.CompilerParams(vmem_limit_bytes=VMEM_LIMIT)
 
 
 def call_back(scale, core, tgt, old, fld):
@@ -146,7 +157,7 @@
             jax.ShapeDtypeStruct((N, N), F32),
             jax.ShapeDtypeStruct((N, N), BF),
         ),
-        in_specs=[SMEM, SMEM, ANY, ANY, ANY],
+        in_specs=[SMEM, SMEM, HBM, HBM, HBM],
         out_specs=(VMEM,) * 4,
         scratch_shapes=[
             pltpu.VMEM((2, N, N), BF),
@@ -155,7 +166,7 @@
             pltpu.VMEM((2, N, N), BF),
             pltpu.SemaphoreType.DMA((3,)),
         ],
-        compiler_params=PARAMS,
+        compiler_params=pltpu.CompilerParams(vmem_limit_bytes=16 * MIB),
         name="back_margin",
     )(scale, core, tgt, old, fld)
 
@@ -168,18 +179,34 @@
             jax.ShapeDtypeStruct((16, 2, 16, N), F32),
             jax.ShapeDtypeStruct((16, 2, 16, N), BF),
         ),
-        in_specs=[SMEM, SMEM, VMEM, VMEM, VMEM, VMEM, ANY, ANY],
+        in_specs=[SMEM, SMEM] + [VMEM] * 6,
         out_specs=(VMEM,) * 3,
-        scratch_shapes=[
-            pltpu.VMEM((2, N, N), BF),
-            pltpu.VMEM((2, N, N), BF),
-            pltpu.VMEM((2, N, N), BF),
-            pltpu.VMEM((2, N, N), BF),
-            pltpu.SemaphoreType.DMA((2,)),
-        ],
-        compiler_params=PARAMS,
+        scratch_shapes=[pltpu.VMEM((2, N, N), BF), pltpu.VMEM((2, N, N), BF)],
+        compiler_params=pltpu.CompilerParams(vmem_limit_bytes=16 * MIB),
         name="ahead_margin",
     )(core, mode, own, other, ar, ai, tgt, fld)
+
+
+def call_power(parts):
+    return pl.pallas_call(
+        power_kernel,
+        out_shape=(jax.ShapeDtypeStruct((2, 16, N), F32), jax.ShapeDtypeStruct((32, 1, 128), F32)),
+        in_specs=[VMEM],
+        out_specs=(VMEM, VMEM),
+        compiler_params=pltpu.CompilerParams(vmem_limit_bytes=8 * MIB),
+        name="row_power",
+    )(parts)
+
+
+def call_phasor(rows, power):
+    return pl.pallas_call(
+        phasor_kernel,
+        out_shape=jax.ShapeDtypeStruct((2, 16, N), BF),
+        in_specs=[VMEM, VMEM],
+        out_specs=VMEM,
+        compiler_params=pltpu.CompilerParams(vmem_limit_bytes=8 * MIB),
+        name="row_phasor",
+    )(rows, power)
 
 
 def exchange(x, axes):
@@ -205,19 +232,15 @@
     mode = lax.axis_index(MODE).reshape(1)
     ar, ai, keep, send = call_back(scales, core, tgt, mask_old, fld)
     half = (keep + swap_cores(send).astype(F32)).astype(BF)
-    part = total_of(exchange(half.reshape(64, 8, N), ("y", "z"))).astype(BF)
-    part = total_of(spread(part, ("xh", "xl"), 4)).astype(BF)
-    own = spread(part, ("y", "z"), 64)
+    part = total_of(exchange(half.reshape(16, 32, N), WAVE)).astype(BF)
+    part = total_of(spread(part, ("y", "xh"), 16)).astype(BF)
+    own = spread(part, WAVE, 16)
     other = swap_cores(own)
     mask_one, keep, send = call_ahead(core, mode, own, other, ar, ai, tgt, fld)
     half = (keep + swap_cores(send).astype(F32)).astype(BF)
     part = total_of(exchange(half, ("y", "xh"))).astype(BF)
-    rows = total_of(spread(part, WAVE, 16))
-    power = jnp.sum(rows * rows)
-    power = spread(jnp.broadcast_to(power.reshape(1, 1), (1, 128)), MODE, 32)
-    power = jnp.sum(power[:, :, :1]) / (N * N)
-    factor = lax.rsqrt(rows[0] * rows[0] + rows[1] * rows[1] + power + 1e-06)
-    return mask_one, (rows * factor[None]).astype(BF)
+    rows, power = call_power(spread(part, WAVE, 16))
+    return mask_one, call_phasor(rows, exchange(power, MODE))
 
 
 def solution(mesh):

time: 156 us -> 159 us (1.019)
  blocking collectives: 113 us -> 121 us
  other arithmetic: 2.53 us -> 0.64 us
  starting transfers between devices: 18.3 us -> 16.5 us
    all_to_all x6, blocking collectives: 113 us -> 121 us  [exchange(): return lax.all_to_all(x, axes, 0, 0, tiled=True)]
    ppermute x3, starting transfers between devices: 18.3 us -> 16.5 us  [swap_cores(): return lax.ppermute(x, 'c', [(0, 1), (1, 0)])]
where the time goes in v2:
time: 159 us
  blocking collectives  121 us (76%)
  starting transfers between devices  16.5 us (10%)
  Pallas kernels  9.2 us (6%)
  local copies, waits for them, and re-layouts  4.86 us (3%)
  waiting for transfers between devices  4.67 us (3%)
    all_to_all x6, blocking collectives, exchange(): return lax.all_to_all(x, axes, 0, 0, tiled=True)  121 us
    ppermute x3, starting transfers between devices, swap_cores(): return lax.ppermute(x, 'c', [(0, 1), (1, 0)])  16.5 us
    unnamed x14, local copies, waits for them, and re-layouts  4.72 us
    pallas_call x1, Pallas kernels, call_ahead(): pl.pallas_call(ahead_kernel, out_shape=(jax.ShapeDtypeStruct((2, 16, N),...  4.7 us
    ppermute x3, waiting for transfers between devices, swap_cores(): return lax.ppermute(x, 'c', [(0, 1), (1, 0)])  4.67 us
    pallas_call x1, Pallas kernels, call_back(): pl.pallas_call(back_kernel, out_shape=(jax.ShapeDtypeStruct((N, N), BF),...  3.57 us
  transfers between devices with their start and end apart: 3, of which 3 were waited for; matrix products, arithmetic and copies ran while one was open for 0% of the time, Pallas kernels for 0%

profile of v2, /device:TPU:1, one launch (start us, length us, event | category | flops | bytes accessed | tf_op | source)
XLA Modules:
  0.0 158.6 jit_solution(1287635288524893126)
XLA Ops:
  1.3 0.0 copy-start
  1.3 1.2 copy-done
  2.5 0.0 copy-start.2
  2.5 1.2 copy-done.2
  3.7 1.2 copy-done.4
  5.0 3.6 %back_margin.1 = (bf16[512,512]{1,0:T(8,128)(2,1)S(1)}, bf16[512,512]{1,0:T(8,128)(2,1)S(1)}, f32[512,512]{1,0:T(8,128)S(1)}, bf16[512,512]{1,0:T(8,128)(2,1)S(1)}) custom-call(f32[1]{0:T(128)S(6)} %copy.6.scale_ref, s32[1]{0:T(128)} %bitcast.core_ref, bf16[2,512,512]{2,1,0:T(8,128)(2,1)S(1)} %bitcast.5, bf16[2,512,512]{2,1,0:T(8,128)(2,1)S(1)} %copy-done.4, ...), custom_call_target="tpu_custom_call" | custom-call | tf_op jit(solution)/shard_map/back_margin/pallas_call | solution.py:152
  8.5 0.0 copy-start.5
  8.5 8.8 %collective-permute-start = (bf16[512,512]{1,0:T(8,128)(2,1)S(1)}, bf16[512,512]{1,0:T(8,128)(2,1)S(1)}, u32[]{:S(2)}, u32[]{:S(2)}) collective-permute-start(bf16[512,512]{1,0:T(8,128)(2,1)S(1)} %get-tuple-element.12), channel_id=1, source_target_pairs={{0,16},{16,0},{1,17},{17,1},{2,18},{18,2},{3,19},{19,3},{4,20},{20... | collective-permute-start | bytes 1572872 | tf_op jit(solution)/shard_map/ppermute | solution.py:225
  17.3 1.5 collective-permute-done
  18.9 0.2 add_convert_fusion.1
  19.1 0.0 copy-done.5
  19.1 19.1 %all_to_all.30 = bf16[16,32,512]{2,1,0:T(8,128)(2,1)S(1)} all-to-all(bf16[16,32,512]{2,1,0:T(8,128)(2,1)S(1)} %bitcast.9), channel_id=1, replica_groups=mesh['y'=8,'xh'=2,'c'=2,'xl'=2,'z'=8] {'xl','z'}, dimensions={0} | all-to-all | bytes 1048576 | tf_op jit(solution)/shard_map/all_to_all | solution.py:213
  38.2 0.1 reduce_sum.36
  38.3 23.8 %all_to_all.31 = bf16[16,32,512]{2,1,0:T(8,128)(2,1)S(1)} all-to-all(bf16[16,32,512]{2,1,0:T(8,128)(2,1)S(1)} %broadcast_in_dim.6), channel_id=1, replica_groups=mesh['y'=8,'xh'=2,'c'=2,'xl'=2,'z'=8] {'y','xh'}, dimensions={0} | all-to-all | bytes 1048576 | tf_op jit(solution)/shard_map/all_to_all | solution.py:213
  62.1 0.1 reduce_sum.37
  62.2 20.8 %all_to_all.32.own = bf16[16,32,512]{2,1,0:T(8,128)(2,1)S(1)} all-to-all(bf16[16,32,512]{2,1,0:T(8,128)(2,1)S(1)} %broadcast_in_dim.7), channel_id=1, replica_groups=mesh['y'=8,'xh'=2,'c'=2,'xl'=2,'z'=8] {'xl','z'}, dimensions={0} | all-to-all | bytes 1048576 | tf_op jit(solution)/shard_map/all_to_all | solution.py:213
  83.0 5.5 %collective-permute-start.1 = (bf16[16,32,512]{2,1,0:T(8,128)(2,1)S(1)}, bf16[16,32,512]{2,1,0:T(8,128)(2,1)}, u32[]{:S(2)}, u32[]{:S(2)}) collective-permute-start(bf16[16,32,512]{2,1,0:T(8,128)(2,1)S(1)} %all_to_all.32.own), channel_id=1, source_target_pairs={{0,16},{16,0},{1,17},{17,1},{2,18},{18,2},{3,19},{19,3},{4,20},{20... | collective-permute-start | bytes 1572872 | tf_op jit(solution)/shard_map/ppermute | solution.py:225
  88.5 1.6 %collective-permute-done.1.other = bf16[16,32,512]{2,1,0:T(8,128)(2,1)} collective-permute-done((bf16[16,32,512]{2,1,0:T(8,128)(2,1)S(1)}, bf16[16,32,512]{2,1,0:T(8,128)(2,1)}, u32[]{:S(2)}, u32[]{:S(2)}) %collective-permute-start.1) | collective-permute-done | bytes 524320 | tf_op jit(solution)/shard_map/ppermute | solution.py:225
  90.2 0.0 copy-done.1
  90.2 0.0 copy-done.3
  90.2 1.0 copy-done.6
  91.2 4.7 %ahead_margin.1 = (bf16[2,16,512]{2,1,0:T(8,128)(2,1)}, f32[16,2,16,512]{3,2,1,0:T(8,128)S(1)}, bf16[16,2,16,512]{3,2,1,0:T(8,128)(2,1)S(1)}) custom-call(s32[1]{0:T(128)} %bitcast.core_ref, s32[1]{0:T(128)} %bitcast.1.mode_ref, bf16[16,32,512]{2,1,0:T(8,128)(2,1)S(1)} %all_to_all.32.own, bf16[16,32,512]{2,1,0:T(8,128)(2,1)} %collective-permute-done.1.other, ...), custom_call_target="tpu_custom_call" | custom-call | tf_op jit(solution)/shard_map/ahead_margin/pallas_call | solution.py:175
  95.9 2.3 %collective-permute-start.2 = (bf16[16,2,16,512]{3,2,1,0:T(8,128)(2,1)S(1)}, bf16[16,2,16,512]{3,2,1,0:T(8,128)(2,1)S(1)}, u32[]{:S(2)}, u32[]{:S(2)}) collective-permute-start(bf16[16,2,16,512]{3,2,1,0:T(8,128)(2,1)S(1)} %get-tuple-element.17), channel_id=1, source_target_pairs={{0,16},{16,0},{1,17},{17,1},{2,18},{18,2},{3,19},{19,3},{4,20},{20... | collective-permute-start | bytes 1572872 | tf_op jit(solution)/shard_map/ppermute | solution.py:225
  98.2 1.5 collective-permute-done.2
  99.7 0.2 add_convert_fusion
  99.9 23.0 %all_to_all.33 = bf16[16,2,16,512]{3,2,1,0:T(8,128)(2,1)S(1)} all-to-all(bf16[16,2,16,512]{3,2,1,0:T(8,128)(2,1)S(1)} %add_convert_fusion), channel_id=1, replica_groups=mesh['y'=8,'xh'=2,'c'=2,'xl'=2,'z'=8] {'y','xh'}, dimensions={0} | all-to-all | bytes 1048576 | tf_op jit(solution)/shard_map/all_to_all | solution.py:213
  122.9 0.1 reduce_sum.38
  123.0 0.1 broadcast_in_dim.8
  123.0 16.5 %all_to_all.34.parts = bf16[16,2,16,512]{3,2,1,0:T(8,128)(2,1)S(1)} all-to-all(bf16[16,2,16,512]{3,2,1,0:T(8,128)(2,1)S(1)} %broadcast_in_dim.8), channel_id=1, replica_groups=mesh['y'=8,'xh'=2,'c'=2,'xl'=2,'z'=8] {'xl','z'}, dimensions={0} | all-to-all | bytes 1048576 | tf_op jit(solution)/shard_map/all_to_all | solution.py:213
  139.5 0.2 row_power.1
  139.7 18.1 %all_to_all.35.power = f32[32,1,128]{2,1,0:T(1,128)S(1)} all-to-all(f32[32,1,128]{2,1,0:T(1,128)S(1)} %get-tuple-element.19), channel_id=1, replica_groups=mesh['y'=8,'xh'=2,'c'=2,'xl'=2,'z'=8] {'y','xh','c'}, dimensions={0} | all-to-all | bytes 32768 | tf_op jit(solution)/shard_map/all_to_all | solution.py:213
  157.9 0.7 row_phasor.1
  (6 shorter events, 0.1 us)
Async XLA Ops:
  1.3 1.2 copy-start
  2.5 1.2 copy-start.2
  3.7 1.2 copy-start.4
  8.5 10.5 %copy-start.5 = (bf16[512,512]{1,0:T(8,128)(2,1)}, bf16[512,512]{1,0:T(8,128)(2,1)S(1)}, u32[]{:S(2)}) copy-start(bf16[512,512]{1,0:T(8,128)(2,1)S(1)} %get-tuple-element.14.ai) | copy-start | bytes 1572868
  8.5 10.3 %collective-permute-start = (bf16[512,512]{1,0:T(8,128)(2,1)S(1)}, bf16[512,512]{1,0:T(8,128)(2,1)S(1)}, u32[]{:S(2)}, u32[]{:S(2)}) collective-permute-start(bf16[512,512]{1,0:T(8,128)(2,1)S(1)} %get-tuple-element.12), channel_id=1, source_target_pairs={{0,16},{16,0},{1,17},{17,1},{2,18},{18,2},{3,19},{19,3},{4,20},{20... | collective-permute-start | bytes 1572872 | tf_op jit(solution)/shard_map/ppermute | solution.py:225
  62.1 28.1 %copy-start.1 = (bf16[1,1,2,512,512]{4,3,2,1,0:T(8,128)(2,1)S(1)}, bf16[1,1,2,512,512]{4,3,2,1,0:T(8,128)(2,1)}, u32[]{:S(2)}) copy-start(bf16[1,1,2,512,512]{4,3,2,1,0:T(8,128)(2,1)} %param.5) | copy-start | bytes 3145732
  62.1 28.1 %copy-start.3 = (bf16[1,1,2,512,512]{4,3,2,1,0:T(8,128)(2,1)S(1)}, bf16[1,1,2,512,512]{4,3,2,1,0:T(8,128)(2,1)}, u32[]{:S(2)}) copy-start(bf16[1,1,2,512,512]{4,3,2,1,0:T(8,128)(2,1)} %param.4) | copy-start | bytes 3145732
  83.0 7.1 %collective-permute-start.1 = (bf16[16,32,512]{2,1,0:T(8,128)(2,1)S(1)}, bf16[16,32,512]{2,1,0:T(8,128)(2,1)}, u32[]{:S(2)}, u32[]{:S(2)}) collective-permute-start(bf16[16,32,512]{2,1,0:T(8,128)(2,1)S(1)} %all_to_all.32.own), channel_id=1, source_target_pairs={{0,16},{16,0},{1,17},{17,1},{2,18},{18,2},{3,19},{19,3},{4,20},{20... | collective-permute-start | bytes 1572872 | tf_op jit(solution)/shard_map/ppermute | solution.py:225
  90.2 1.0 copy-start.6
  95.9 3.8 %collective-permute-start.2 = (bf16[16,2,16,512]{3,2,1,0:T(8,128)(2,1)S(1)}, bf16[16,2,16,512]{3,2,1,0:T(8,128)(2,1)S(1)}, u32[]{:S(2)}, u32[]{:S(2)}) collective-permute-start(bf16[16,2,16,512]{3,2,1,0:T(8,128)(2,1)S(1)} %get-tuple-element.17), channel_id=1, source_target_pairs={{0,16},{16,0},{1,17},{17,1},{2,18},{18,2},{3,19},{19,3},{4,20},{20... | collective-permute-start | bytes 1572872 | tf_op jit(solution)/shard_map/ppermute | solution.py:225

commit v3 on v2

--- a/solution.py
+++ b/solution.py
@@ -115,32 +115,43 @@
         bi = tgt[1, rows].astype(F32)
         term_r = br * ahead_r + bi * ahead_i
         term_i = bi * ahead_r - br * ahead_i
-        for q in range(BLK // 32):
-            for part, term in ((0, term_r), (1, term_i)):
-                even = term[q * 32 : q * 32 + 16]
-                odd = term[q * 32 + 16 : q * 32 + 32]
-                keep[r // 32 + q, part] = jnp.where(first, even, odd)
-                send[r // 32 + q, part] = jnp.where(first, odd, even).astype(BF)
-
-
-def power_kernel(parts, rows, power):
+        for low in range(BLK // 32):
+            q = r // 32 + low
+            for w in range(16):
+                part, half, col = w // 8, w // 4 % 2, w % 4
+                term = (term_r, term_i)[part][:, col * 128 : (col + 1) * 128]
+                even = term[low * 32 + half * 8 : low * 32 + half * 8 + 8]
+                odd = term[low * 32 + 16 + half * 8 : low * 32 + 24 + half * 8]
+                i = jnp.where(first, q, w)
+                j = jnp.where(first, w, q)
+                keep[i, j] = jnp.where(first, even, odd)
+                send[j, i] = jnp.where(first, odd, even).astype(BF)
+
+
+def power_kernel(mode_ref, parts, tiles, message):
     total = parts[0].astype(F32)
-    for w in range(1, 16):
-        total = total + parts[w].astype(F32)
-    rows[...] = total
-    power[...] = jnp.broadcast_to(jnp.sum(total * total), (32, 1, 128))
-
-
-def phasor_kernel(rows, power, out):
-    total = power[0]
-    for w in range(1, 32):
-        total = total + power[w]
-    bias = total[:, :1] / (N * N) + 1e-06
-    a = rows[0]
-    b = rows[1]
-    factor = lax.rsqrt(a * a + b * b + bias)
-    out[0] = (a * factor).astype(BF)
-    out[1] = (b * factor).astype(BF)
+    for k in range(1, 16):
+        total = total + parts[k].astype(F32)
+    tiles[...] = total
+    power = jnp.broadcast_to(jnp.sum(total * total), (8, 128))
+    mine = tiles[mode_ref[0] // 2]
+    for k in range(16):
+        message[k, 0:8] = mine
+        message[k, 8:16] = power
+
+
+def phasor_kernel(core_ref, tiles, arrived, power, other, out, full):
+    first = core_ref[0] == 0
+    bias = (power[...] + other[...]) / (N * N) + 1e-06
+    for half in range(2):
+        for col in range(4):
+            k = half * 4 + col
+            a = jnp.where(first, tiles[k], arrived[k, 0:8])
+            b = jnp.where(first, tiles[k + 8], arrived[k + 8, 0:8])
+            factor = lax.rsqrt(a * a + b * b + bias)
+            full[0, half * 8 : half * 8 + 8, col * 128 : (col + 1) * 128] = a * factor
+            full[1, half * 8 : half * 8 + 8, col * 128 : (col + 1) * 128] = b * factor
+    out[...] = full[...].astype(BF)
 
 
 HBM = pl.BlockSpec(memory_space=pltpu.HBM)
@@ -176,8 +187,8 @@
         ahead_kernel,
         out_shape=(
             jax.ShapeDtypeStruct((2, 16, N), BF),
-            jax.ShapeDtypeStruct((16, 2, 16, N), F32),
-            jax.ShapeDtypeStruct((16, 2, 16, N), BF),
+            jax.ShapeDtypeStruct((16, 16, 8, 128), F32),
+            jax.ShapeDtypeStruct((16, 16, 8, 128), BF),
         ),
         in_specs=[SMEM, SMEM] + [VMEM] * 6,
         out_specs=(VMEM,) * 3,
@@ -187,38 +198,54 @@
     )(core, mode, own, other, ar, ai, tgt, fld)
 
 
-def call_power(parts):
+def call_power(mode, parts):
     return pl.pallas_call(
         power_kernel,
-        out_shape=(jax.ShapeDtypeStruct((2, 16, N), F32), jax.ShapeDtypeStruct((32, 1, 128), F32)),
-        in_specs=[VMEM],
+        out_shape=(jax.ShapeDtypeStruct((16, 8, 128), F32), jax.ShapeDtypeStruct((16, 16, 128), F32)),
+        in_specs=[SMEM, VMEM],
         out_specs=(VMEM, VMEM),
         compiler_params=pltpu.CompilerParams(vmem_limit_bytes=8 * MIB),
-        name="row_power",
-    )(parts)
-
-
-def call_phasor(rows, power):
+        name="tile_power",
+    )(mode, parts)
+
+
+def call_phasor(core, tiles, arrived, power, other):
     return pl.pallas_call(
         phasor_kernel,
         out_shape=jax.ShapeDtypeStruct((2, 16, N), BF),
-        in_specs=[VMEM, VMEM],
+        in_specs=[SMEM] + [VMEM] * 4,
         out_specs=VMEM,
+        scratch_shapes=[pltpu.VMEM((2, 16, N), F32)],
         compiler_params=pltpu.CompilerParams(vmem_limit_bytes=8 * MIB),
-        name="row_phasor",
-    )(rows, power)
-
-
-def exchange(x, axes):
-    return lax.all_to_all(x, axes, 0, 0, tiled=True)
-
-
-def spread(x, axes, count):
-    return exchange(jnp.broadcast_to(x[None], (count,) + x.shape), axes)
+        name="tile_phasor",
+    )(core, tiles, arrived, power, other)
+
+
+def device(y, xh, c, xl, z):
+    return (((y * 2 + xh) * 2 + c) * 2 + xl) * 8 + z
+
+
+def ring_groups(core):
+    rows = [(y, xh) for y in range(8) for xh in range(2)]
+    waves = [(xl, z) for xl in range(2) for z in range(8)]
+    groups = [[device(*q, core, *w) for q in rows] for w in waves]
+    return groups + [[device(*q, 1 - core, *w) for w in waves] for q in rows]
+
+
+RING_A = ring_groups(0)
+RING_B = ring_groups(1)
+
+
+def exchange(x, groups):
+    return lax.all_to_all(x, AXES, 0, 0, tiled=True, axis_index_groups=groups)
+
+
+def spread(x, groups):
+    return exchange(jnp.broadcast_to(x[None], (16,) + x.shape), groups)
 
 
 def total_of(x):
-    return jnp.sum(x.astype(F32), 0)
+    return jnp.sum(x.astype(F32), 0).astype(BF)
 
 
 def swap_cores(x):
@@ -232,15 +259,17 @@
     mode = lax.axis_index(MODE).reshape(1)
     ar, ai, keep, send = call_back(scales, core, tgt, mask_old, fld)
     half = (keep + swap_cores(send).astype(F32)).astype(BF)
-    part = total_of(exchange(half.reshape(16, 32, N), WAVE)).astype(BF)
-    part = total_of(spread(part, ("y", "xh"), 16)).astype(BF)
-    own = spread(part, WAVE, 16)
+    part = total_of(exchange(half.reshape(16, 32, N), RING_A))
+    part = total_of(spread(part, RING_B))
+    own = spread(part, RING_A)
     other = swap_cores(own)
     mask_one, keep, send = call_ahead(core, mode, own, other, ar, ai, tgt, fld)
     half = (keep + swap_cores(send).astype(F32)).astype(BF)
-    part = total_of(exchange(half, ("y", "xh"))).astype(BF)
-    rows, power = call_power(spread(part, WAVE, 16))
-    return mask_one, call_phasor(rows, exchange(power, MODE))
+    part = total_of(exchange(half, RING_A))
+    tiles, message = call_power(mode, spread(part, RING_B))
+    arrived = exchange(message, RING_A)
+    power = jnp.sum(arrived[:, 8:], 0)
+    return mask_one, call_phasor(core, tiles, arrived, power, swap_cores(power))
 
 
 def solution(mesh):

time: 159 us -> 144 us (0.906)
  blocking collectives: 121 us -> 95.6 us
  starting transfers between devices: 16.5 us -> 26.2 us
    all_to_all x6, blocking collectives: 121 us -> 95.6 us  [exchange(): return lax.all_to_all(x, AXES, 0, 0, tiled=True, axis_index_groups=groups)]
    ppermute x3 -> x4, starting transfers between devices: 16.5 us -> 26.2 us  [swap_cores(): return lax.ppermute(x, 'c', [(0, 1), (1, 0)])]
    ppermute x3 -> x4, waiting for transfers between devices: 4.67 us -> 5.47 us  [swap_cores(): return lax.ppermute(x, 'c', [(0, 1), (1, 0)])]
  transfers between devices with their start and end apart: 3 -> 4, of which waited for: 3 -> 4; matrix products, arithmetic and copies ran while one was open for 0% -> 0% of each run, Pallas kernels for 0% -> 0%
where the time goes in v3:
time: 144 us
  blocking collectives  95.6 us (66%)
  starting transfers between devices  26.2 us (18%)
  Pallas kernels  9.38 us (7%)
  waiting for transfers between devices  5.47 us (4%)
  local copies, waits for them, and re-layouts  4.91 us (3%)
    all_to_all x6, blocking collectives, exchange(): return lax.all_to_all(x, AXES, 0, 0, tiled=True, axis_index_groups=groups)  95.6 us
    ppermute x4, starting transfers between devices, swap_cores(): return lax.ppermute(x, 'c', [(0, 1), (1, 0)])  26.2 us
    ppermute x4, waiting for transfers between devices, swap_cores(): return lax.ppermute(x, 'c', [(0, 1), (1, 0)])  5.47 us
    pallas_call x1, Pallas kernels, call_ahead(): pl.pallas_call(ahead_kernel, out_shape=(jax.ShapeDtypeStruct((2, 16, N),...  4.98 us
    unnamed x14, local copies, waits for them, and re-layouts  4.72 us
    pallas_call x1, Pallas kernels, call_back(): pl.pallas_call(back_kernel, out_shape=(jax.ShapeDtypeStruct((N, N), BF),...  3.57 us
  transfers between devices with their start and end apart: 4, of which 4 were waited for; matrix products, arithmetic and copies ran while one was open for 0% of the time, Pallas kernels for 0%

profile of v3, /device:TPU:1, one launch (start us, length us, event | category | flops | bytes accessed | tf_op | source)
XLA Modules:
  0.0 143.5 jit_solution(13408563143830116996)
XLA Ops:
  1.3 0.0 copy-start
  1.3 1.2 copy-done
  2.5 1.2 copy-done.2
  3.7 1.2 copy-done.4
  5.0 3.6 %back_margin.1 = (bf16[512,512]{1,0:T(8,128)(2,1)S(1)}, bf16[512,512]{1,0:T(8,128)(2,1)S(1)}, f32[512,512]{1,0:T(8,128)S(1)}, bf16[512,512]{1,0:T(8,128)(2,1)S(1)}) custom-call(f32[1]{0:T(128)S(6)} %copy.6.scale_ref, s32[1]{0:T(128)} %bitcast.core_ref, bf16[2,512,512]{2,1,0:T(8,128)(2,1)S(1)} %bitcast.5, bf16[2,512,512]{2,1,0:T(8,128)(2,1)S(1)} %copy-done.4, ...), custom_call_target="tpu_custom_call" | custom-call | tf_op jit(solution)/shard_map/back_margin/pallas_call | solution.py:163
  8.5 0.0 copy-start.5
  8.5 8.8 %collective-permute-start = (bf16[512,512]{1,0:T(8,128)(2,1)S(1)}, bf16[512,512]{1,0:T(8,128)(2,1)S(1)}, u32[]{:S(2)}, u32[]{:S(2)}) collective-permute-start(bf16[512,512]{1,0:T(8,128)(2,1)S(1)} %get-tuple-element.12), channel_id=1, source_target_pairs={{0,16},{16,0},{1,17},{17,1},{2,18},{18,2},{3,19},{19,3},{4,20},{20... | collective-permute-start | bytes 1572872 | tf_op jit(solution)/shard_map/ppermute | solution.py:252
  17.3 1.5 %collective-permute-done = bf16[512,512]{1,0:T(8,128)(2,1)S(1)} collective-permute-done((bf16[512,512]{1,0:T(8,128)(2,1)S(1)}, bf16[512,512]{1,0:T(8,128)(2,1)S(1)}, u32[]{:S(2)}, u32[]{:S(2)}) %collective-permute-start) | collective-permute-done | bytes 524320 | tf_op jit(solution)/shard_map/ppermute | solution.py:252
  18.9 0.2 add_convert_fusion.1
  19.1 0.0 copy-done.5
  19.1 16.1 %all_to_all.30 = bf16[16,32,512]{2,1,0:T(8,128)(2,1)S(1)} all-to-all(bf16[16,32,512]{2,1,0:T(8,128)(2,1)S(1)} %bitcast.9), channel_id=1, replica_groups={{0,32,64,96,128,160,192,224,256,288,320,352,384,416,448,480},{1,33,65,9..., dimensions={0} | all-to-all | bytes 1048576 | tf_op jit(solution)/shard_map/all_to_all | solution.py:240
  35.2 0.1 reduce_sum.45
  35.3 22.0 %all_to_all.31 = bf16[16,32,512]{2,1,0:T(8,128)(2,1)S(1)} all-to-all(bf16[16,32,512]{2,1,0:T(8,128)(2,1)S(1)} %broadcast_in_dim.6), channel_id=1, replica_groups={{16,48,80,112,144,176,208,240,272,304,336,368,400,432,464,496},{17,49,8..., dimensions={0} | all-to-all | bytes 1048576 | tf_op jit(solution)/shard_map/all_to_all | solution.py:240
  57.3 0.1 reduce_sum.46
  57.4 15.2 %all_to_all.32.own = bf16[16,32,512]{2,1,0:T(8,128)(2,1)S(1)} all-to-all(bf16[16,32,512]{2,1,0:T(8,128)(2,1)S(1)} %broadcast_in_dim.7), channel_id=1, replica_groups={{0,32,64,96,128,160,192,224,256,288,320,352,384,416,448,480},{1,33,65,9..., dimensions={0} | all-to-all | bytes 1048576 | tf_op jit(solution)/shard_map/all_to_all | solution.py:240
  72.6 7.5 %collective-permute-start.1 = (bf16[16,32,512]{2,1,0:T(8,128)(2,1)S(1)}, bf16[16,32,512]{2,1,0:T(8,128)(2,1)}, u32[]{:S(2)}, u32[]{:S(2)}) collective-permute-start(bf16[16,32,512]{2,1,0:T(8,128)(2,1)S(1)} %all_to_all.32.own), channel_id=1, source_target_pairs={{0,16},{16,0},{1,17},{17,1},{2,18},{18,2},{3,19},{19,3},{4,20},{20... | collective-permute-start | bytes 1572872 | tf_op jit(solution)/shard_map/ppermute | solution.py:252
  80.0 1.6 %collective-permute-done.1.other = bf16[16,32,512]{2,1,0:T(8,128)(2,1)} collective-permute-done((bf16[16,32,512]{2,1,0:T(8,128)(2,1)S(1)}, bf16[16,32,512]{2,1,0:T(8,128)(2,1)}, u32[]{:S(2)}, u32[]{:S(2)}) %collective-permute-start.1) | collective-permute-done | bytes 524320 | tf_op jit(solution)/shard_map/ppermute | solution.py:252
  81.7 0.0 copy-done.1
  81.7 1.0 copy-done.6
  82.7 5.0 %ahead_margin.1 = (bf16[2,16,512]{2,1,0:T(8,128)(2,1)}, f32[16,16,8,128]{3,2,1,0:T(8,128)S(1)}, bf16[16,16,8,128]{3,2,1,0:T(8,128)(2,1)S(1)}) custom-call(s32[1]{0:T(128)} %bitcast.core_ref, s32[1]{0:T(128)} %bitcast.1.mode_ref, bf16[16,32,512]{2,1,0:T(8,128)(2,1)S(1)} %all_to_all.32.own, bf16[16,32,512]{2,1,0:T(8,128)(2,1)} %collective-permute-done.1.other, ...), custom_call_target="tpu_custom_call" | custom-call | tf_op jit(solution)/shard_map/ahead_margin/pallas_call | solution.py:186
  87.7 2.3 %collective-permute-start.2 = (bf16[16,16,8,128]{3,2,1,0:T(8,128)(2,1)S(1)}, bf16[16,16,8,128]{3,2,1,0:T(8,128)(2,1)S(1)}, u32[]{:S(2)}, u32[]{:S(2)}) collective-permute-start(bf16[16,16,8,128]{3,2,1,0:T(8,128)(2,1)S(1)} %get-tuple-element.17), channel_id=1, source_target_pairs={{0,16},{16,0},{1,17},{17,1},{2,18},{18,2},{3,19},{19,3},{4,20},{20... | collective-permute-start | bytes 1572872 | tf_op jit(solution)/shard_map/ppermute | solution.py:252
  90.0 1.5 %collective-permute-done.2 = bf16[16,16,8,128]{3,2,1,0:T(8,128)(2,1)S(1)} collective-permute-done((bf16[16,16,8,128]{3,2,1,0:T(8,128)(2,1)S(1)}, bf16[16,16,8,128]{3,2,1,0:T(8,128)(2,1)S(1)}, u32[]{:S(2)}, u32[]{:S(2)}) %collective-permute-start.2) | collective-permute-done | bytes 524320 | tf_op jit(solution)/shard_map/ppermute | solution.py:252
  91.5 0.1 add_convert_fusion
  91.7 14.1 %all_to_all.33 = bf16[16,16,8,128]{3,2,1,0:T(8,128)(2,1)S(1)} all-to-all(bf16[16,16,8,128]{3,2,1,0:T(8,128)(2,1)S(1)} %add_convert_fusion), channel_id=1, replica_groups={{0,32,64,96,128,160,192,224,256,288,320,352,384,416,448,480},{1,33,65,9..., dimensions={0} | all-to-all | bytes 1048576 | tf_op jit(solution)/shard_map/all_to_all | solution.py:240
  105.8 0.1 reduce_sum.47
  105.9 0.1 broadcast_in_dim.8
  106.0 16.5 %all_to_all.34.parts = bf16[16,16,8,128]{3,2,1,0:T(8,128)(2,1)S(1)} all-to-all(bf16[16,16,8,128]{3,2,1,0:T(8,128)(2,1)S(1)} %broadcast_in_dim.8), channel_id=1, replica_groups={{16,48,80,112,144,176,208,240,272,304,336,368,400,432,464,496},{17,49,8..., dimensions={0} | all-to-all | bytes 1048576 | tf_op jit(solution)/shard_map/all_to_all | solution.py:240
  122.5 0.2 tile_power.1
  122.7 11.7 %all_to_all.35.arrived = f32[16,16,128]{2,1,0:T(8,128)S(1)} all-to-all(f32[16,16,128]{2,1,0:T(8,128)S(1)} %get-tuple-element.19), channel_id=1, replica_groups={{0,32,64,96,128,160,192,224,256,288,320,352,384,416,448,480},{1,33,65,9..., dimensions={0} | all-to-all | bytes 262144 | tf_op jit(solution)/shard_map/all_to_all | solution.py:240
  134.4 7.7 %collective-permute-start.3 = (f32[8,128]{1,0:T(8,128)S(1)}, f32[8,128]{1,0:T(8,128)S(1)}, u32[]{:S(2)}, u32[]{:S(2)}) collective-permute-start(f32[8,128]{1,0:T(8,128)S(1)} %slice_reduce_fusion.power), channel_id=1, source_target_pairs={{0,16},{16,0},{1,17},{17,1},{2,18},{18,2},{3,19},{19,3},{4,20},{20... | collective-permute-start | bytes 12296 | tf_op jit(solution)/shard_map/ppermute | solution.py:252
  142.1 0.8 collective-permute-done.3.other
  142.9 0.6 tile_phasor.1
  (9 shorter events, 0.1 us)
Async XLA Ops:
  1.3 1.2 copy-start
  2.5 1.2 copy-start.2
  3.7 1.2 copy-start.4
  8.5 10.5 %copy-start.5 = (bf16[512,512]{1,0:T(8,128)(2,1)}, bf16[512,512]{1,0:T(8,128)(2,1)S(1)}, u32[]{:S(2)}) copy-start(bf16[512,512]{1,0:T(8,128)(2,1)S(1)} %get-tuple-element.14.ai) | copy-start | bytes 1572868
  8.5 10.3 %collective-permute-start = (bf16[512,512]{1,0:T(8,128)(2,1)S(1)}, bf16[512,512]{1,0:T(8,128)(2,1)S(1)}, u32[]{:S(2)}, u32[]{:S(2)}) collective-permute-start(bf16[512,512]{1,0:T(8,128)(2,1)S(1)} %get-tuple-element.12), channel_id=1, source_target_pairs={{0,16},{16,0},{1,17},{17,1},{2,18},{18,2},{3,19},{19,3},{4,20},{20... | collective-permute-start | bytes 1572872 | tf_op jit(solution)/shard_map/ppermute | solution.py:252
  57.3 24.4 %copy-start.1 = (bf16[1,1,2,512,512]{4,3,2,1,0:T(8,128)(2,1)S(1)}, bf16[1,1,2,512,512]{4,3,2,1,0:T(8,128)(2,1)}, u32[]{:S(2)}) copy-start(bf16[1,1,2,512,512]{4,3,2,1,0:T(8,128)(2,1)} %param.5) | copy-start | bytes 3145732
  57.3 24.4 %copy-start.3 = (bf16[1,1,2,512,512]{4,3,2,1,0:T(8,128)(2,1)S(1)}, bf16[1,1,2,512,512]{4,3,2,1,0:T(8,128)(2,1)}, u32[]{:S(2)}) copy-start(bf16[1,1,2,512,512]{4,3,2,1,0:T(8,128)(2,1)} %param.4) | copy-start | bytes 3145732
  72.6 9.1 %collective-permute-start.1 = (bf16[16,32,512]{2,1,0:T(8,128)(2,1)S(1)}, bf16[16,32,512]{2,1,0:T(8,128)(2,1)}, u32[]{:S(2)}, u32[]{:S(2)}) collective-permute-start(bf16[16,32,512]{2,1,0:T(8,128)(2,1)S(1)} %all_to_all.32.own), channel_id=1, source_target_pairs={{0,16},{16,0},{1,17},{17,1},{2,18},{18,2},{3,19},{19,3},{4,20},{20... | collective-permute-start | bytes 1572872 | tf_op jit(solution)/shard_map/ppermute | solution.py:252
  81.7 1.0 copy-start.6
  87.7 3.8 %collective-permute-start.2 = (bf16[16,16,8,128]{3,2,1,0:T(8,128)(2,1)S(1)}, bf16[16,16,8,128]{3,2,1,0:T(8,128)(2,1)S(1)}, u32[]{:S(2)}, u32[]{:S(2)}) collective-permute-start(bf16[16,16,8,128]{3,2,1,0:T(8,128)(2,1)S(1)} %get-tuple-element.17), channel_id=1, source_target_pairs={{0,16},{16,0},{1,17},{17,1},{2,18},{18,2},{3,19},{19,3},{4,20},{20... | collective-permute-start | bytes 1572872 | tf_op jit(solution)/shard_map/ppermute | solution.py:252
  134.4 8.5 %collective-permute-start.3 = (f32[8,128]{1,0:T(8,128)S(1)}, f32[8,128]{1,0:T(8,128)S(1)}, u32[]{:S(2)}, u32[]{:S(2)}) collective-permute-start(f32[8,128]{1,0:T(8,128)S(1)} %slice_reduce_fusion.power), channel_id=1, source_target_pairs={{0,16},{16,0},{1,17},{17,1},{2,18},{18,2},{3,19},{19,3},{4,20},{20... | collective-permute-start | bytes 12296 | tf_op jit(solution)/shard_map/ppermute | solution.py:252

commit v4 on v3

--- a/solution.py
+++ b/solution.py
@@ -14,6 +14,7 @@
 WAVE = ("xl", "z")
 MIB = 1024 * 1024
 BLK = 128
+CHUNK = 16
 
 
 def dot(a, b):
@@ -39,16 +40,23 @@
                     ref[row * BLK : (row + 1) * BLK, col * BLK : (col + 1) * BLK] = block
 
 
-def back_kernel(scale_ref, core_ref, tgt_hbm, old_hbm, fld_hbm, ar, ai, keep, send, tgt, old, fld, z_s, sems):
-    copies = [
-        pltpu.make_async_copy(src, dst, sems.at[i])
+def chirp_kernel(scale_ref, after, a):
+    chirp_into(scale_ref[0], a.at[0], a.at[1])
+
+
+def back_kernel(scale_ref, core_ref, tgt_hbm, old_hbm, fld_hbm, keep_hbm, send_hbm,
+                tgt, old, fld, a, z_s, keep, send, in_sems, out_sems):
+    arrive = [
+        pltpu.make_async_copy(src.at[part], dst.at[part], in_sems.at[2 * i + part])
         for i, (src, dst) in enumerate(((tgt_hbm, tgt), (old_hbm, old), (fld_hbm, fld)))
+        for part in range(2)
     ]
-    for copy in copies:
+    for copy in arrive:
         copy.start()
-    chirp_into(scale_ref[0], ar, ai)
-    copies[0].wait()
-    copies[1].wait()
+    chirp_into(scale_ref[0], a.at[0], a.at[1])
+    leave = []
+    for copy in arrive[:4]:
+        copy.wait()
     for r in range(0, N, BLK):
         rows = slice(r, r + BLK)
         br = tgt[0, rows].astype(F32)
@@ -57,36 +65,43 @@
         mi = old[1, rows].astype(F32)
         cr = (br * mr + bi * mi).astype(BF)
         ci = (bi * mr - br * mi).astype(BF)
-        z_s[0, rows] = (dot(cr, ar[...]) + dot(ci, ai[...])).astype(BF)
-        z_s[1, rows] = (dot(ci, ar[...]) - dot(cr, ai[...])).astype(BF)
-    copies[2].wait()
+        z_s[0, rows] = (dot(cr, a[0]) + dot(ci, a[1])).astype(BF)
+        z_s[1, rows] = (dot(ci, a[0]) - dot(cr, a[1])).astype(BF)
+    for copy in arrive[4:]:
+        copy.wait()
     first = core_ref[0] == 0
     for r in range(0, N, BLK):
         rows = slice(r, r + BLK)
-        kr = ar[rows]
-        ki = ai[rows]
+        kr = a[0, rows]
+        ki = a[1, rows]
         back_r = dot(kr, z_s[0]) + dot(ki, z_s[1])
         back_i = dot(kr, z_s[1]) - dot(ki, z_s[0])
         fr = fld[0, rows].astype(F32)
         fi = fld[1, rows].astype(F32)
         term_r = back_r * fr + back_i * fi
         term_i = back_i * fr - back_r * fi
-        keep[rows] = jnp.where(first, term_r, term_i)
         send[rows] = jnp.where(first, term_i, term_r).astype(BF)
-
-
-def ahead_kernel(core_ref, mode_ref, own, other, ar, ai, tgt, fld, mask_out, keep, send, mask, z_s):
+        keep[rows] = jnp.where(first, term_r, term_i).astype(BF)
+        for src, dst in ((send, send_hbm), (keep, keep_hbm)):
+            copy = pltpu.make_async_copy(src.at[rows], dst.at[rows], out_sems.at[len(leave)])
+            copy.start()
+            leave.append(copy)
+    for copy in leave:
+        copy.wait()
+
+
+def ahead_kernel(core_ref, mode_ref, own, other, a_ref, tgt, fld, mask_out, keep, send, mask, z_s):
     first = core_ref[0] == 0
-    total = jnp.zeros((32, N), F32)
-    for r in range(16):
+    total = jnp.zeros((CHUNK, N), F32)
+    for r in range(N // CHUNK):
         a = own[r].astype(F32)
         b = other[r].astype(F32)
         total = total + (a * a + b * b)
     bias = jnp.sum(total) / (N * N) + 1e-06
     for r in range(0, N, BLK):
         rows = slice(r, r + BLK)
-        a = own[r // 32 : (r + BLK) // 32].reshape(BLK, N).astype(F32)
-        b = other[r // 32 : (r + BLK) // 32].reshape(BLK, N).astype(F32)
+        a = own[r // CHUNK : (r + BLK) // CHUNK].reshape(BLK, N).astype(F32)
+        b = other[r // CHUNK : (r + BLK) // CHUNK].reshape(BLK, N).astype(F32)
         factor = lax.rsqrt(a * a + b * b + bias)
         a = a * factor
         b = b * factor
@@ -100,15 +115,15 @@
         fi = fld[1, rows].astype(F32)
         gr = (fr * mr - fi * mi).astype(BF)
         gi = (fr * mi + fi * mr).astype(BF)
-        z_s[0, rows] = (dot(gr, ar[...]) - dot(gi, ai[...])).astype(BF)
-        z_s[1, rows] = (dot(gi, ar[...]) + dot(gr, ai[...])).astype(BF)
+        z_s[0, rows] = (dot(gr, a_ref[0]) - dot(gi, a_ref[1])).astype(BF)
+        z_s[1, rows] = (dot(gi, a_ref[0]) + dot(gr, a_ref[1])).astype(BF)
     start = pl.multiple_of(mode_ref[0] * 16, 16)
     mask_out[0] = mask[0, pl.ds(start, 16)]
     mask_out[1] = mask[1, pl.ds(start, 16)]
     for r in range(0, N, BLK):
         rows = slice(r, r + BLK)
-        kr = ar[rows]
-        ki = ai[rows]
+        kr = a_ref[0, rows]
+        ki = a_ref[1, rows]
         ahead_r = dot(kr, z_s[0]) - dot(ki, z_s[1])
         ahead_i = dot(kr, z_s[1]) + dot(ki, z_s[0])
         br = tgt[0, rows].astype(F32)
@@ -134,20 +149,22 @@
         total = total + parts[k].astype(F32)
     tiles[...] = total
     power = jnp.broadcast_to(jnp.sum(total * total), (8, 128))
-    mine = tiles[mode_ref[0] // 2]
+    high = power.astype(BF).astype(F32)
+    row = lax.broadcasted_iota(jnp.int32, (8, 128), 0)
+    power = jnp.where(row < 4, high, power - high)
+    mine = jnp.concatenate([tiles[mode_ref[0] // 2], power], 0).astype(BF)
     for k in range(16):
-        message[k, 0:8] = mine
-        message[k, 8:16] = power
+        message[k] = mine
 
 
 def phasor_kernel(core_ref, tiles, arrived, power, other, out, full):
     first = core_ref[0] == 0
-    bias = (power[...] + other[...]) / (N * N) + 1e-06
+    bias = jnp.sum(power[...] + other[...], 0, keepdims=True) / (4 * N * N) + 1e-06
     for half in range(2):
         for col in range(4):
             k = half * 4 + col
-            a = jnp.where(first, tiles[k], arrived[k, 0:8])
-            b = jnp.where(first, tiles[k + 8], arrived[k + 8, 0:8])
+            a = jnp.where(first, tiles[k], arrived[k].astype(F32)[0:8])
+            b = jnp.where(first, tiles[k + 8], arrived[k + 8].astype(F32)[0:8])
             factor = lax.rsqrt(a * a + b * b + bias)
             full[0, half * 8 : half * 8 + 8, col * 128 : (col + 1) * 128] = a * factor
             full[1, half * 8 : half * 8 + 8, col * 128 : (col + 1) * 128] = b * factor
@@ -155,34 +172,46 @@
 
 
 HBM = pl.BlockSpec(memory_space=pltpu.HBM)
+ANY = pl.BlockSpec(memory_space=pl.ANY)
 SMEM = pl.BlockSpec(memory_space=pltpu.SMEM)
 VMEM = pl.BlockSpec(memory_space=pltpu.VMEM)
 
 
+def call_chirp(scale, after):
+    return pl.pallas_call(
+        chirp_kernel,
+        out_shape=jax.ShapeDtypeStruct((2, N, N), BF),
+        in_specs=[SMEM, ANY],
+        out_specs=VMEM,
+        compiler_params=pltpu.CompilerParams(vmem_limit_bytes=8 * MIB),
+        cost_estimate=pl.CostEstimate(flops=10**9, bytes_accessed=2**20, transcendentals=2**12),
+        name="chirp",
+    )(scale, after)
+
+
 def call_back(scale, core, tgt, old, fld):
+    blocks = N // BLK
     return pl.pallas_call(
         back_kernel,
         out_shape=(
             jax.ShapeDtypeStruct((N, N), BF),
             jax.ShapeDtypeStruct((N, N), BF),
-            jax.ShapeDtypeStruct((N, N), F32),
-            jax.ShapeDtypeStruct((N, N), BF),
         ),
         in_specs=[SMEM, SMEM, HBM, HBM, HBM],
-        out_specs=(VMEM,) * 4,
-        scratch_shapes=[
-            pltpu.VMEM((2, N, N), BF),
-            pltpu.VMEM((2, N, N), BF),
-            pltpu.VMEM((2, N, N), BF),
-            pltpu.VMEM((2, N, N), BF),
-            pltpu.SemaphoreType.DMA((3,)),
+        out_specs=(HBM,) * 2,
+        scratch_shapes=[pltpu.VMEM((2, N, N), BF)] * 5
+        + [
+            pltpu.VMEM((N, N), BF),
+            pltpu.VMEM((N, N), BF),
+            pltpu.SemaphoreType.DMA((6,)),
+            pltpu.SemaphoreType.DMA((2 * blocks,)),
         ],
-        compiler_params=pltpu.CompilerParams(vmem_limit_bytes=16 * MIB),
+        compiler_params=pltpu.CompilerParams(vmem_limit_bytes=58 * MIB),
         name="back_margin",
     )(scale, core, tgt, old, fld)
 
 
-def call_ahead(core, mode, own, other, ar, ai, tgt, fld):
+def call_ahead(core, mode, own, other, a, tgt, fld):
     return pl.pallas_call(
         ahead_kernel,
         out_shape=(
@@ -190,18 +219,18 @@
             jax.ShapeDtypeStruct((16, 16, 8, 128), F32),
             jax.ShapeDtypeStruct((16, 16, 8, 128), BF),
         ),
-        in_specs=[SMEM, SMEM] + [VMEM] * 6,
+        in_specs=[SMEM, SMEM] + [VMEM] * 5,
         out_specs=(VMEM,) * 3,
         scratch_shapes=[pltpu.VMEM((2, N, N), BF), pltpu.VMEM((2, N, N), BF)],
         compiler_params=pltpu.CompilerParams(vmem_limit_bytes=16 * MIB),
         name="ahead_margin",
-    )(core, mode, own, other, ar, ai, tgt, fld)
+    )(core, mode, own, other, a, tgt, fld)
 
 
 def call_power(mode, parts):
     return pl.pallas_call(
         power_kernel,
-        out_shape=(jax.ShapeDtypeStruct((16, 8, 128), F32), jax.ShapeDtypeStruct((16, 16, 128), F32)),
+        out_shape=(jax.ShapeDtypeStruct((16, 8, 128), F32), jax.ShapeDtypeStruct((16, 16, 128), BF)),
         in_specs=[SMEM, VMEM],
         out_specs=(VMEM, VMEM),
         compiler_params=pltpu.CompilerParams(vmem_limit_bytes=8 * MIB),
@@ -225,15 +254,40 @@
     return (((y * 2 + xh) * 2 + c) * 2 + xl) * 8 + z
 
 
-def ring_groups(core):
-    rows = [(y, xh) for y in range(8) for xh in range(2)]
-    waves = [(xl, z) for xl in range(2) for z in range(8)]
-    groups = [[device(*q, core, *w) for q in rows] for w in waves]
-    return groups + [[device(*q, 1 - core, *w) for w in waves] for q in rows]
-
-
-RING_A = ring_groups(0)
-RING_B = ring_groups(1)
+def ring_groups(core, rows, waves):
+    def groups(own, cross, c, make):
+        return [[device(**make(i, j), c=c) for i in own] for j in cross]
+
+    flat = lambda i, j: {**i, **j}
+    return groups(rows, waves, core, flat) + groups(waves, rows, 1 - core, flat)
+
+
+def points(**sizes):
+    found = [{}]
+    for name, size in sizes.items():
+        found = [{**point, name: k} for point in found for k in range(size)]
+    return found
+
+
+def wide_groups():
+    x = points(xh=2, xl=2)
+    y, z = points(y=8), points(z=8)
+    first = [[device(**i, **k, **j, c=0) for i in y for k in x] for j in z]
+    return first + [[device(**i, **k, **j, c=1) for j in z for k in x] for i in y]
+
+
+def narrow_groups():
+    x = points(xh=2, xl=2)
+    y, z = points(y=8), points(z=8)
+    first = [[device(**i, **k, **j, c=0) for j in z] for i in y for k in x]
+    return first + [[device(**i, **k, **j, c=1) for i in y] for j in z for k in x]
+
+
+ROWS, WAVES = points(y=8, xh=2), points(xl=2, z=8)
+RING_A = ring_groups(0, ROWS, WAVES)
+RING_B = ring_groups(1, ROWS, WAVES)
+WIDE = wide_groups()
+NARROW = narrow_groups()
 
 
 def exchange(x, groups):
@@ -241,7 +295,7 @@
 
 
 def spread(x, groups):
-    return exchange(jnp.broadcast_to(x[None], (16,) + x.shape), groups)
+    return exchange(jnp.broadcast_to(x[None], (len(groups[0]),) + x.shape), groups)
 
 
 def total_of(x):
@@ -257,18 +311,19 @@
     tgt = target[0, 0]
     core = lax.axis_index("c").reshape(1)
     mode = lax.axis_index(MODE).reshape(1)
-    ar, ai, keep, send = call_back(scales, core, tgt, mask_old, fld)
-    half = (keep + swap_cores(send).astype(F32)).astype(BF)
-    part = total_of(exchange(half.reshape(16, 32, N), RING_A))
-    part = total_of(spread(part, RING_B))
-    own = spread(part, RING_A)
+    keep, send = call_back(scales, core, tgt, mask_old, fld)
+    half = (keep.astype(F32) + swap_cores(send).astype(F32)).astype(BF)
+    part = total_of(exchange(half.reshape(N // CHUNK, CHUNK, N), WIDE))
+    part = total_of(spread(part, NARROW))
+    own = spread(part, WIDE)
     other = swap_cores(own)
-    mask_one, keep, send = call_ahead(core, mode, own, other, ar, ai, tgt, fld)
+    a = call_chirp(scales, own)
+    mask_one, keep, send = call_ahead(core, mode, own, other, a, tgt, fld)
     half = (keep + swap_cores(send).astype(F32)).astype(BF)
     part = total_of(exchange(half, RING_A))
     tiles, message = call_power(mode, spread(part, RING_B))
     arrived = exchange(message, RING_A)
-    power = jnp.sum(arrived[:, 8:], 0)
+    power = jnp.sum(arrived[:, 8:].astype(F32), 0)
     return mask_one, call_phasor(core, tiles, arrived, power, swap_cores(power))
 
 

time: 144 us -> 136 us (0.944)
  local copies, waits for them, and re-layouts: 4.91 us -> 0.21 us
  blocking collectives: 95.6 us -> 93 us
  starting transfers between devices: 26.2 us -> 23.9 us
    unnamed x14 -> x4, local copies, waits for them, and re-layouts: 4.72 us -> 0.05 us
    all_to_all x6, blocking collectives: 95.6 us -> 93 us  [exchange(): return lax.all_to_all(x, AXES, 0, 0, tiled=True, axis_index_groups=groups)]
    ppermute x4, starting transfers between devices: 26.2 us -> 23.9 us  [swap_cores(): return lax.ppermute(x, 'c', [(0, 1), (1, 0)])]
    pallas_call x1, Pallas kernels: 3.57 us -> 5.31 us  [call_back(): pl.pallas_call(back_kernel, out_shape=(jax.ShapeDtypeStruct((N, N), BF),...]
where the time goes in v4:
time: 136 us
  blocking collectives  93 us (68%)
  starting transfers between devices  23.9 us (18%)
  Pallas kernels  10.7 us (8%)
  waiting for transfers between devices  5.23 us (4%)
  other arithmetic  1.52 us (1%)
  between operations  1.4 us (1%)
    all_to_all x6, blocking collectives, exchange(): return lax.all_to_all(x, AXES, 0, 0, tiled=True, axis_index_groups=groups)  93 us
    ppermute x4, starting transfers between devices, swap_cores(): return lax.ppermute(x, 'c', [(0, 1), (1, 0)])  23.9 us
    pallas_call x1, Pallas kernels, call_back(): pl.pallas_call(back_kernel, out_shape=(jax.ShapeDtypeStruct((N, N), BF),...  5.31 us
    ppermute x4, waiting for transfers between devices, swap_cores(): return lax.ppermute(x, 'c', [(0, 1), (1, 0)])  5.23 us
    pallas_call x1, Pallas kernels, call_ahead(): pl.pallas_call(ahead_kernel, out_shape=(jax.ShapeDtypeStruct((2, 16, N),...  4.24 us
  transfers between devices with their start and end apart: 4, of which 4 were waited for; matrix products, arithmetic and copies ran while one was open for 0% of the time, Pallas kernels for 0%

profile of v4, /device:TPU:1, one launch (start us, length us, event | category | flops | bytes accessed | tf_op | source)
XLA Modules:
  0.0 136.0 jit_solution(3315856230106825928)
XLA Ops:
  1.3 5.3 %back_margin.1 = (bf16[512,512]{1,0:T(8,128)(2,1)}, bf16[512,512]{1,0:T(8,128)(2,1)}) custom-call(f32[1]{0:T(128)S(6)} %copy.6.scale_ref, s32[1]{0:T(128)} %bitcast.core_ref, bf16[2,512,512]{2,1,0:T(8,128)(2,1)} %bitcast.5, bf16[2,512,512]{2,1,0:T(8,128)(2,1)} %old_hbm.1, bf16[2,512,512]{2,1,0:T(8,128)(2,1)} %bitcast.7), custom_call_target="tpu_custom_call" | custom-call | tf_op jit(solution)/shard_map/back_margin/pallas_call | solution.py:194
  6.6 8.8 %collective-permute-start = (bf16[512,512]{1,0:T(8,128)(2,1)}, bf16[512,512]{1,0:T(8,128)(2,1)S(1)}, u32[]{:S(2)}, u32[]{:S(2)}) collective-permute-start(bf16[512,512]{1,0:T(8,128)(2,1)} %get-tuple-element.10), channel_id=1, source_target_pairs={{0,16},{16,0},{1,17},{17,1},{2,18},{18,2},{3,19},{19,3},{4,20},{20... | collective-permute-start | bytes 1572872 | tf_op jit(solution)/shard_map/ppermute | solution.py:306
  15.4 1.7 %collective-permute-done = bf16[512,512]{1,0:T(8,128)(2,1)S(1)} collective-permute-done((bf16[512,512]{1,0:T(8,128)(2,1)}, bf16[512,512]{1,0:T(8,128)(2,1)S(1)}, u32[]{:S(2)}, u32[]{:S(2)}) %collective-permute-start) | collective-permute-done | bytes 524320 | tf_op jit(solution)/shard_map/ppermute | solution.py:306
  17.1 1.2 add_convert_fusion.1
  18.3 20.0 %all_to_all.30 = bf16[32,16,512]{2,1,0:T(8,128)(2,1)S(1)} all-to-all(bf16[32,16,512]{2,1,0:T(8,128)(2,1)S(1)} %bitcast.9), channel_id=1, replica_groups={{0,8,32,40,64,72,96,104,128,136,160,168,192,200,224,232,256,264,288,296..., dimensions={0} | all-to-all | bytes 1048576 | tf_op jit(solution)/shard_map/all_to_all | solution.py:294
  38.3 0.1 reduce_sum.45
  38.4 14.5 %all_to_all.31 = bf16[8,16,512]{2,1,0:T(8,128)(2,1)S(1)} all-to-all(bf16[8,16,512]{2,1,0:T(8,128)(2,1)S(1)} %broadcast_in_dim.6), channel_id=1, replica_groups={{0,1,2,3,4,5,6,7},{8,9,10,11,12,13,14,15},{32,33,34,35,36,37,38,39},{40..., dimensions={0} | all-to-all | bytes 262144 | tf_op jit(solution)/shard_map/all_to_all | solution.py:294
  53.0 0.1 broadcast_in_dim.7
  53.0 16.9 %all_to_all.32.after.own = bf16[32,16,512]{2,1,0:T(8,128)(2,1)S(1)} all-to-all(bf16[32,16,512]{2,1,0:T(8,128)(2,1)S(1)} %broadcast_in_dim.7), channel_id=1, replica_groups={{0,8,32,40,64,72,96,104,128,136,160,168,192,200,224,232,256,264,288,296..., dimensions={0} | all-to-all | bytes 1048576 | tf_op jit(solution)/shard_map/all_to_all | solution.py:294
  69.9 6.2 %collective-permute-start.1 = (bf16[32,16,512]{2,1,0:T(8,128)(2,1)S(1)}, bf16[32,16,512]{2,1,0:T(8,128)(2,1)S(1)}, u32[]{:S(2)}, u32[]{:S(2)}) collective-permute-start(bf16[32,16,512]{2,1,0:T(8,128)(2,1)S(1)} %all_to_all.32.after.own), channel_id=1, source_target_pairs={{0,16},{16,0},{1,17},{17,1},{2,18},{18,2},{3,19},{19,3},{4,20},{20... | collective-permute-start | bytes 1572872 | tf_op jit(solution)/shard_map/ppermute | solution.py:306
  76.2 0.0 copy-start
  76.2 0.0 copy-start.1
  76.2 0.3 chirp.1.a_ref
  76.5 1.2 collective-permute-done.1.other
  77.7 0.0 copy-done
  77.7 0.0 copy-done.1
  77.7 4.2 %ahead_margin.1 = (bf16[2,16,512]{2,1,0:T(8,128)(2,1)}, f32[16,16,8,128]{3,2,1,0:T(8,128)S(1)}, bf16[16,16,8,128]{3,2,1,0:T(8,128)(2,1)S(1)}) custom-call(s32[1]{0:T(128)} %bitcast.core_ref, s32[1]{0:T(128)} %bitcast.1.mode_ref, bf16[32,16,512]{2,1,0:T(8,128)(2,1)S(1)} %all_to_all.32.after.own, bf16[32,16,512]{2,1,0:T(8,128)(2,1)S(1)} %collective-permute-done.1.other, ...), custom_call_target="tpu_custom_call" | custom-call | tf_op jit(solution)/shard_map/ahead_margin/pallas_call | solution.py:215
  82.0 2.2 %collective-permute-start.2 = (bf16[16,16,8,128]{3,2,1,0:T(8,128)(2,1)S(1)}, bf16[16,16,8,128]{3,2,1,0:T(8,128)(2,1)S(1)}, u32[]{:S(2)}, u32[]{:S(2)}) collective-permute-start(bf16[16,16,8,128]{3,2,1,0:T(8,128)(2,1)S(1)} %get-tuple-element.13), channel_id=1, source_target_pairs={{0,16},{16,0},{1,17},{17,1},{2,18},{18,2},{3,19},{19,3},{4,20},{20... | collective-permute-start | bytes 1572872 | tf_op jit(solution)/shard_map/ppermute | solution.py:306
  84.2 1.6 %collective-permute-done.2 = bf16[16,16,8,128]{3,2,1,0:T(8,128)(2,1)S(1)} collective-permute-done((bf16[16,16,8,128]{3,2,1,0:T(8,128)(2,1)S(1)}, bf16[16,16,8,128]{3,2,1,0:T(8,128)(2,1)S(1)}, u32[]{:S(2)}, u32[]{:S(2)}) %collective-permute-start.2) | collective-permute-done | bytes 524320 | tf_op jit(solution)/shard_map/ppermute | solution.py:306
  85.8 0.1 add_convert_fusion
  85.9 13.2 %all_to_all.33 = bf16[16,16,8,128]{3,2,1,0:T(8,128)(2,1)S(1)} all-to-all(bf16[16,16,8,128]{3,2,1,0:T(8,128)(2,1)S(1)} %add_convert_fusion), channel_id=1, replica_groups={{0,32,64,96,128,160,192,224,256,288,320,352,384,416,448,480},{1,33,65,9..., dimensions={0} | all-to-all | bytes 1048576 | tf_op jit(solution)/shard_map/all_to_all | solution.py:294
  99.1 0.1 reduce_sum.47
  99.2 0.1 broadcast_in_dim.8
  99.3 17.1 %all_to_all.34.parts = bf16[16,16,8,128]{3,2,1,0:T(8,128)(2,1)S(1)} all-to-all(bf16[16,16,8,128]{3,2,1,0:T(8,128)(2,1)S(1)} %broadcast_in_dim.8), channel_id=1, replica_groups={{16,48,80,112,144,176,208,240,272,304,336,368,400,432,464,496},{17,49,8..., dimensions={0} | all-to-all | bytes 1048576 | tf_op jit(solution)/shard_map/all_to_all | solution.py:294
  116.4 0.2 tile_power.1
  116.6 11.3 %all_to_all.35.arrived = bf16[16,16,128]{2,1,0:T(8,128)(2,1)S(1)} all-to-all(bf16[16,16,128]{2,1,0:T(8,128)(2,1)S(1)} %get-tuple-element.15), channel_id=1, replica_groups={{0,32,64,96,128,160,192,224,256,288,320,352,384,416,448,480},{1,33,65,9..., dimensions={0} | all-to-all | bytes 131072 | tf_op jit(solution)/shard_map/all_to_all | solution.py:294
  127.9 6.6 %collective-permute-start.3 = (f32[8,128]{1,0:T(8,128)S(1)}, f32[8,128]{1,0:T(8,128)S(1)}, u32[]{:S(2)}, u32[]{:S(2)}) collective-permute-start(f32[8,128]{1,0:T(8,128)S(1)} %convert_reduce_fusion.power), channel_id=1, source_target_pairs={{0,16},{16,0},{1,17},{17,1},{2,18},{18,2},{3,19},{19,3},{4,20},{20... | collective-permute-start | bytes 12296 | tf_op jit(solution)/shard_map/ppermute | solution.py:306
  134.5 0.8 collective-permute-done.3.other
  135.3 0.6 tile_phasor.1
  (3 shorter events, 0.1 us)
Async XLA Ops:
  6.6 10.5 %collective-permute-start = (bf16[512,512]{1,0:T(8,128)(2,1)}, bf16[512,512]{1,0:T(8,128)(2,1)S(1)}, u32[]{:S(2)}, u32[]{:S(2)}) collective-permute-start(bf16[512,512]{1,0:T(8,128)(2,1)} %get-tuple-element.10), channel_id=1, source_target_pairs={{0,16},{16,0},{1,17},{17,1},{2,18},{18,2},{3,19},{19,3},{4,20},{20... | collective-permute-start | bytes 1572872 | tf_op jit(solution)/shard_map/ppermute | solution.py:306
  69.9 7.8 %collective-permute-start.1 = (bf16[32,16,512]{2,1,0:T(8,128)(2,1)S(1)}, bf16[32,16,512]{2,1,0:T(8,128)(2,1)S(1)}, u32[]{:S(2)}, u32[]{:S(2)}) collective-permute-start(bf16[32,16,512]{2,1,0:T(8,128)(2,1)S(1)} %all_to_all.32.after.own), channel_id=1, source_target_pairs={{0,16},{16,0},{1,17},{17,1},{2,18},{18,2},{3,19},{19,3},{4,20},{20... | collective-permute-start | bytes 1572872 | tf_op jit(solution)/shard_map/ppermute | solution.py:306
  76.2 1.5 %copy-start = (bf16[1,1,2,512,512]{4,3,2,1,0:T(8,128)(2,1)S(1)}, bf16[1,1,2,512,512]{4,3,2,1,0:T(8,128)(2,1)}, u32[]{:S(2)}) copy-start(bf16[1,1,2,512,512]{4,3,2,1,0:T(8,128)(2,1)} %param.5) | copy-start | bytes 3145732
  76.2 1.5 %copy-start.1 = (bf16[1,1,2,512,512]{4,3,2,1,0:T(8,128)(2,1)S(1)}, bf16[1,1,2,512,512]{4,3,2,1,0:T(8,128)(2,1)}, u32[]{:S(2)}) copy-start(bf16[1,1,2,512,512]{4,3,2,1,0:T(8,128)(2,1)} %param.4) | copy-start | bytes 3145732
  82.0 3.8 %collective-permute-start.2 = (bf16[16,16,8,128]{3,2,1,0:T(8,128)(2,1)S(1)}, bf16[16,16,8,128]{3,2,1,0:T(8,128)(2,1)S(1)}, u32[]{:S(2)}, u32[]{:S(2)}) collective-permute-start(bf16[16,16,8,128]{3,2,1,0:T(8,128)(2,1)S(1)} %get-tuple-element.13), channel_id=1, source_target_pairs={{0,16},{16,0},{1,17},{17,1},{2,18},{18,2},{3,19},{19,3},{4,20},{20... | collective-permute-start | bytes 1572872 | tf_op jit(solution)/shard_map/ppermute | solution.py:306
  127.9 7.4 %collective-permute-start.3 = (f32[8,128]{1,0:T(8,128)S(1)}, f32[8,128]{1,0:T(8,128)S(1)}, u32[]{:S(2)}, u32[]{:S(2)}) collective-permute-start(f32[8,128]{1,0:T(8,128)S(1)} %convert_reduce_fusion.power), channel_id=1, source_target_pairs={{0,16},{16,0},{1,17},{17,1},{2,18},{18,2},{3,19},{19,3},{4,20},{20... | collective-permute-start | bytes 12296 | tf_op jit(solution)/shard_map/ppermute | solution.py:306

commit v5 on v4

--- a/solution.py
+++ b/solution.py
@@ -44,21 +44,19 @@
     chirp_into(scale_ref[0], a.at[0], a.at[1])
 
 
-def back_kernel(scale_ref, core_ref, tgt_hbm, old_hbm, fld_hbm, keep_hbm, send_hbm,
-                tgt, old, fld, a, z_s, keep, send, in_sems, out_sems):
-    arrive = [
-        pltpu.make_async_copy(src.at[part], dst.at[part], in_sems.at[2 * i + part])
-        for i, (src, dst) in enumerate(((tgt_hbm, tgt), (old_hbm, old), (fld_hbm, fld)))
-        for part in range(2)
-    ]
+def back_kernel(scale_ref, core_ref, tgt_hbm, old_hbm, fld_hbm, keep, send, tgt, old, fld, a, z_s, sems):
+    blocks = [slice(r, r + BLK) for r in range(0, N, BLK)]
+    arrive = []
+    for pairs in (((tgt_hbm, tgt), (old_hbm, old)), ((fld_hbm, fld),)):
+        for rows in blocks:
+            for src, dst in pairs:
+                arrive.append(pltpu.make_async_copy(src.at[:, rows], dst.at[:, rows], sems.at[len(arrive)]))
     for copy in arrive:
         copy.start()
     chirp_into(scale_ref[0], a.at[0], a.at[1])
-    leave = []
-    for copy in arrive[:4]:
-        copy.wait()
-    for r in range(0, N, BLK):
-        rows = slice(r, r + BLK)
+    for i, rows in enumerate(blocks):
+        arrive[2 * i].wait()
+        arrive[2 * i + 1].wait()
         br = tgt[0, rows].astype(F32)
         bi = tgt[1, rows].astype(F32)
         mr = old[0, rows].astype(F32)
@@ -67,30 +65,44 @@
         ci = (bi * mr - br * mi).astype(BF)
         z_s[0, rows] = (dot(cr, a[0]) + dot(ci, a[1])).astype(BF)
         z_s[1, rows] = (dot(ci, a[0]) - dot(cr, a[1])).astype(BF)
-    for copy in arrive[4:]:
-        copy.wait()
     first = core_ref[0] == 0
-    for r in range(0, N, BLK):
-        rows = slice(r, r + BLK)
+    for i, rows in enumerate(blocks):
         kr = a[0, rows]
         ki = a[1, rows]
         back_r = dot(kr, z_s[0]) + dot(ki, z_s[1])
         back_i = dot(kr, z_s[1]) - dot(ki, z_s[0])
+        arrive[2 * len(blocks) + i].wait()
         fr = fld[0, rows].astype(F32)
         fi = fld[1, rows].astype(F32)
         term_r = back_r * fr + back_i * fi
         term_i = back_i * fr - back_r * fi
         send[rows] = jnp.where(first, term_i, term_r).astype(BF)
         keep[rows] = jnp.where(first, term_r, term_i).astype(BF)
-        for src, dst in ((send, send_hbm), (keep, keep_hbm)):
-            copy = pltpu.make_async_copy(src.at[rows], dst.at[rows], out_sems.at[len(leave)])
-            copy.start()
-            leave.append(copy)
-    for copy in leave:
-        copy.wait()
-
-
-def ahead_kernel(core_ref, mode_ref, own, other, a_ref, tgt, fld, mask_out, keep, send, mask, z_s):
+
+
+def ahead_rows(owner, by_mode, a_ref, z_s, tgt, out):
+    def gather(ref, part, first_q):
+        starts = [pl.multiple_of(32 * (first_q + k) + 16 * owner, 16) for k in range(8)]
+        return jnp.concatenate([ref[part, pl.ds(start, 16)] for start in starts], 0)
+
+    for first_q in (0, 8):
+        kr = gather(a_ref, 0, first_q)
+        ki = gather(a_ref, 1, first_q)
+        ahead_r = dot(kr, z_s[0]) - dot(ki, z_s[1])
+        ahead_i = dot(kr, z_s[1]) + dot(ki, z_s[0])
+        br = gather(tgt, 0, first_q).astype(F32)
+        bi = gather(tgt, 1, first_q).astype(F32)
+        terms = (br * ahead_r + bi * ahead_i, bi * ahead_r - br * ahead_i)
+        for low in range(8):
+            q = first_q + low
+            for w in range(16):
+                part, half, col = w // 8, w // 4 % 2, w % 4
+                top = low * 16 + half * 8
+                tile = terms[part][top : top + 8, col * 128 : (col + 1) * 128]
+                out[jnp.where(by_mode, q, w), jnp.where(by_mode, w, q)] = tile.astype(out.dtype)
+
+
+def ahead_kernel(core_ref, mode_ref, own, other, a_ref, tgt, fld, mask_out, z_s, send, mask):
     first = core_ref[0] == 0
     total = jnp.zeros((CHUNK, N), F32)
     for r in range(N // CHUNK):
@@ -120,27 +132,11 @@
     start = pl.multiple_of(mode_ref[0] * 16, 16)
     mask_out[0] = mask[0, pl.ds(start, 16)]
     mask_out[1] = mask[1, pl.ds(start, 16)]
-    for r in range(0, N, BLK):
-        rows = slice(r, r + BLK)
-        kr = a_ref[0, rows]
-        ki = a_ref[1, rows]
-        ahead_r = dot(kr, z_s[0]) - dot(ki, z_s[1])
-        ahead_i = dot(kr, z_s[1]) + dot(ki, z_s[0])
-        br = tgt[0, rows].astype(F32)
-        bi = tgt[1, rows].astype(F32)
-        term_r = br * ahead_r + bi * ahead_i
-        term_i = bi * ahead_r - br * ahead_i
-        for low in range(BLK // 32):
-            q = r // 32 + low
-            for w in range(16):
-                part, half, col = w // 8, w // 4 % 2, w % 4
-                term = (term_r, term_i)[part][:, col * 128 : (col + 1) * 128]
-                even = term[low * 32 + half * 8 : low * 32 + half * 8 + 8]
-                odd = term[low * 32 + 16 + half * 8 : low * 32 + 24 + half * 8]
-                i = jnp.where(first, q, w)
-                j = jnp.where(first, w, q)
-                keep[i, j] = jnp.where(first, even, odd)
-                send[j, i] = jnp.where(first, odd, even).astype(BF)
+    ahead_rows(1 - core_ref[0], core_ref[0] != 0, a_ref, z_s, tgt, send)
+
+
+def keep_kernel(core_ref, a_ref, z_s, tgt, keep):
+    ahead_rows(core_ref[0], core_ref[0] == 0, a_ref, z_s, tgt, keep)
 
 
 def power_kernel(mode_ref, parts, tiles, message):
@@ -198,15 +194,12 @@
             jax.ShapeDtypeStruct((N, N), BF),
         ),
         in_specs=[SMEM, SMEM, HBM, HBM, HBM],
-        out_specs=(HBM,) * 2,
+        out_specs=(VMEM,) * 2,
         scratch_shapes=[pltpu.VMEM((2, N, N), BF)] * 5
         + [
-            pltpu.VMEM((N, N), BF),
-            pltpu.VMEM((N, N), BF),
-            pltpu.SemaphoreType.DMA((6,)),
-            pltpu.SemaphoreType.DMA((2 * blocks,)),
+            pltpu.SemaphoreType.DMA((3 * blocks,)),
         ],
-        compiler_params=pltpu.CompilerParams(vmem_limit_bytes=58 * MIB),
+        compiler_params=pltpu.CompilerParams(vmem_limit_bytes=52 * MIB),
         name="back_margin",
     )(scale, core, tgt, old, fld)
 
@@ -216,15 +209,27 @@
         ahead_kernel,
         out_shape=(
             jax.ShapeDtypeStruct((2, 16, N), BF),
-            jax.ShapeDtypeStruct((16, 16, 8, 128), F32),
+            jax.ShapeDtypeStruct((2, N, N), BF),
             jax.ShapeDtypeStruct((16, 16, 8, 128), BF),
         ),
         in_specs=[SMEM, SMEM] + [VMEM] * 5,
         out_specs=(VMEM,) * 3,
-        scratch_shapes=[pltpu.VMEM((2, N, N), BF), pltpu.VMEM((2, N, N), BF)],
+        scratch_shapes=[pltpu.VMEM((2, N, N), BF)],
         compiler_params=pltpu.CompilerParams(vmem_limit_bytes=16 * MIB),
         name="ahead_margin",
     )(core, mode, own, other, a, tgt, fld)
+
+
+def call_keep(core, a, z, tgt):
+    return pl.pallas_call(
+        keep_kernel,
+        out_shape=jax.ShapeDtypeStruct((16, 16, 8, 128), F32),
+        in_specs=[SMEM] + [VMEM] * 3,
+        out_specs=VMEM,
+        compiler_params=pltpu.CompilerParams(vmem_limit_bytes=16 * MIB),
+        cost_estimate=pl.CostEstimate(flops=2**30, bytes_accessed=2**22, transcendentals=0),
+        name="keep_margin",
+    )(core, a, z, tgt)
 
 
 def call_power(mode, parts):
@@ -318,8 +323,10 @@
     own = spread(part, WIDE)
     other = swap_cores(own)
     a = call_chirp(scales, own)
-    mask_one, keep, send = call_ahead(core, mode, own, other, a, tgt, fld)
-    half = (keep + swap_cores(send).astype(F32)).astype(BF)
+    mask_one, middle, send = call_ahead(core, mode, own, other, a, tgt, fld)
+    came = swap_cores(send)
+    keep = call_keep(core, a, middle, tgt)
+    half = (keep + came.astype(F32)).astype(BF)
     part = total_of(exchange(half, RING_A))
     tiles, message = call_power(mode, spread(part, RING_B))
     arrived = exchange(message, RING_A)

time: 136 us -> 134 us (0.985)
  transfers between devices with their start and end apart: 4 -> 4, of which waited for: 4 -> 4; matrix products, arithmetic and copies ran while one was open for 0% -> 0% of each run, Pallas kernels for 0% -> 1%
where the time goes in v5:
time: 134 us
  blocking collectives  93 us (69%)
  starting transfers between devices  23.9 us (18%)
  Pallas kernels  11 us (8%)
  waiting for transfers between devices  4.03 us (3%)
  between operations  1.41 us (1%)
    all_to_all x6, blocking collectives, exchange(): return lax.all_to_all(x, AXES, 0, 0, tiled=True, axis_index_groups=groups)  93 us
    ppermute x4, starting transfers between devices, swap_cores(): return lax.ppermute(x, 'c', [(0, 1), (1, 0)])  23.9 us
    pallas_call x1, Pallas kernels, call_back(): pl.pallas_call(back_kernel, out_shape=(jax.ShapeDtypeStruct((N, N), BF),...  5.33 us
    ppermute x4, waiting for transfers between devices, swap_cores(): return lax.ppermute(x, 'c', [(0, 1), (1, 0)])  4.03 us
    pallas_call x1, Pallas kernels, call_ahead(): pl.pallas_call(ahead_kernel, out_shape=(jax.ShapeDtypeStruct((2, 16, N),...  3.52 us
  transfers between devices with their start and end apart: 4, of which 4 were waited for; matrix products, arithmetic and copies ran while one was open for 0% of the time, Pallas kernels for 1%

profile of v5, /device:TPU:1, one launch (start us, length us, event | category | flops | bytes accessed | tf_op | source)
XLA Modules:
  0.0 134.0 jit_solution(14041174181936073087)
XLA Ops:
  1.3 5.3 %back_margin.1 = (bf16[512,512]{1,0:T(8,128)(2,1)S(1)}, bf16[512,512]{1,0:T(8,128)(2,1)S(1)}) custom-call(f32[1]{0:T(128)S(6)} %copy.6.scale_ref, s32[1]{0:T(128)} %bitcast.core_ref, bf16[2,512,512]{2,1,0:T(8,128)(2,1)} %bitcast.5, bf16[2,512,512]{2,1,0:T(8,128)(2,1)} %old_hbm.1, bf16[2,512,512]{2,1,0:T(8,128)(2,1)} %bitcast.8), custom_call_target="tpu_custom_call" | custom-call | tf_op jit(solution)/shard_map/back_margin/pallas_call | solution.py:190
  6.6 8.8 %collective-permute-start = (bf16[512,512]{1,0:T(8,128)(2,1)S(1)}, bf16[512,512]{1,0:T(8,128)(2,1)S(1)}, u32[]{:S(2)}, u32[]{:S(2)}) collective-permute-start(bf16[512,512]{1,0:T(8,128)(2,1)S(1)} %get-tuple-element.10), channel_id=1, source_target_pairs={{0,16},{16,0},{1,17},{17,1},{2,18},{18,2},{3,19},{19,3},{4,20},{20... | collective-permute-start | bytes 1572872 | tf_op jit(solution)/shard_map/ppermute | solution.py:311
  15.4 1.5 %collective-permute-done = bf16[512,512]{1,0:T(8,128)(2,1)S(1)} collective-permute-done((bf16[512,512]{1,0:T(8,128)(2,1)S(1)}, bf16[512,512]{1,0:T(8,128)(2,1)S(1)}, u32[]{:S(2)}, u32[]{:S(2)}) %collective-permute-start) | collective-permute-done | bytes 524320 | tf_op jit(solution)/shard_map/ppermute | solution.py:311
  16.9 0.1 add_convert_fusion.1
  17.1 20.0 %all_to_all.30 = bf16[32,16,512]{2,1,0:T(8,128)(2,1)S(1)} all-to-all(bf16[32,16,512]{2,1,0:T(8,128)(2,1)S(1)} %bitcast.10), channel_id=1, replica_groups={{0,8,32,40,64,72,96,104,128,136,160,168,192,200,224,232,256,264,288,296..., dimensions={0} | all-to-all | bytes 1048576 | tf_op jit(solution)/shard_map/all_to_all | solution.py:299
  37.1 0.1 reduce_sum.45
  37.2 14.5 %all_to_all.31 = bf16[8,16,512]{2,1,0:T(8,128)(2,1)S(1)} all-to-all(bf16[8,16,512]{2,1,0:T(8,128)(2,1)S(1)} %broadcast_in_dim.6), channel_id=1, replica_groups={{0,1,2,3,4,5,6,7},{8,9,10,11,12,13,14,15},{32,33,34,35,36,37,38,39},{40..., dimensions={0} | all-to-all | bytes 262144 | tf_op jit(solution)/shard_map/all_to_all | solution.py:299
  51.7 0.1 broadcast_in_dim.7
  51.8 16.9 %all_to_all.32.after.own = bf16[32,16,512]{2,1,0:T(8,128)(2,1)S(1)} all-to-all(bf16[32,16,512]{2,1,0:T(8,128)(2,1)S(1)} %broadcast_in_dim.7), channel_id=1, replica_groups={{0,8,32,40,64,72,96,104,128,136,160,168,192,200,224,232,256,264,288,296..., dimensions={0} | all-to-all | bytes 1048576 | tf_op jit(solution)/shard_map/all_to_all | solution.py:299
  68.7 6.2 %collective-permute-start.1 = (bf16[32,16,512]{2,1,0:T(8,128)(2,1)S(1)}, bf16[32,16,512]{2,1,0:T(8,128)(2,1)S(1)}, u32[]{:S(2)}, u32[]{:S(2)}) collective-permute-start(bf16[32,16,512]{2,1,0:T(8,128)(2,1)S(1)} %all_to_all.32.after.own), channel_id=1, source_target_pairs={{0,16},{16,0},{1,17},{17,1},{2,18},{18,2},{3,19},{19,3},{4,20},{20... | collective-permute-start | bytes 1572872 | tf_op jit(solution)/shard_map/ppermute | solution.py:311
  74.9 0.0 copy-start
  74.9 0.0 copy-start.1
  75.0 0.3 chirp.1.a_ref
  75.3 1.2 collective-permute-done.1.other
  76.4 0.0 copy-done
  76.4 0.0 copy-done.1
  76.5 3.5 %ahead_margin.1 = (bf16[2,16,512]{2,1,0:T(8,128)(2,1)}, bf16[2,512,512]{2,1,0:T(8,128)(2,1)S(1)}, bf16[16,16,8,128]{3,2,1,0:T(8,128)(2,1)S(1)}) custom-call(s32[1]{0:T(128)} %bitcast.core_ref, s32[1]{0:T(128)} %bitcast.1.mode_ref, bf16[32,16,512]{2,1,0:T(8,128)(2,1)S(1)} %all_to_all.32.after.own, bf16[32,16,512]{2,1,0:T(8,128)(2,1)S(1)} %collective-permute-done.1.other, ...), custom_call_target="tpu_custom_call" | custom-call | tf_op jit(solution)/shard_map/ahead_margin/pallas_call | solution.py:208
  80.0 2.2 %collective-permute-start.2 = (bf16[16,16,8,128]{3,2,1,0:T(8,128)(2,1)S(1)}, bf16[16,16,8,128]{3,2,1,0:T(8,128)(2,1)S(1)}, u32[]{:S(2)}, u32[]{:S(2)}) collective-permute-start(bf16[16,16,8,128]{3,2,1,0:T(8,128)(2,1)S(1)} %get-tuple-element.13), channel_id=1, source_target_pairs={{0,16},{16,0},{1,17},{17,1},{2,18},{18,2},{3,19},{19,3},{4,20},{20... | collective-permute-start | bytes 1572872 | tf_op jit(solution)/shard_map/ppermute | solution.py:311
  82.2 1.0 keep_margin.1
  83.2 0.6 collective-permute-done.2
  83.8 0.2 add_convert_fusion
  84.0 13.2 %all_to_all.33 = bf16[16,16,8,128]{3,2,1,0:T(8,128)(2,1)S(1)} all-to-all(bf16[16,16,8,128]{3,2,1,0:T(8,128)(2,1)S(1)} %add_convert_fusion), channel_id=1, replica_groups={{0,32,64,96,128,160,192,224,256,288,320,352,384,416,448,480},{1,33,65,9..., dimensions={0} | all-to-all | bytes 1048576 | tf_op jit(solution)/shard_map/all_to_all | solution.py:299
  97.1 0.1 reduce_sum.47
  97.2 0.1 broadcast_in_dim.8
  97.3 17.1 %all_to_all.34.parts = bf16[16,16,8,128]{3,2,1,0:T(8,128)(2,1)S(1)} all-to-all(bf16[16,16,8,128]{3,2,1,0:T(8,128)(2,1)S(1)} %broadcast_in_dim.8), channel_id=1, replica_groups={{16,48,80,112,144,176,208,240,272,304,336,368,400,432,464,496},{17,49,8..., dimensions={0} | all-to-all | bytes 1048576 | tf_op jit(solution)/shard_map/all_to_all | solution.py:299
  114.4 0.2 tile_power.1
  114.6 11.3 %all_to_all.35.arrived = bf16[16,16,128]{2,1,0:T(8,128)(2,1)S(1)} all-to-all(bf16[16,16,128]{2,1,0:T(8,128)(2,1)S(1)} %get-tuple-element.15), channel_id=1, replica_groups={{0,32,64,96,128,160,192,224,256,288,320,352,384,416,448,480},{1,33,65,9..., dimensions={0} | all-to-all | bytes 131072 | tf_op jit(solution)/shard_map/all_to_all | solution.py:299
  125.9 6.6 %collective-permute-start.3 = (f32[8,128]{1,0:T(8,128)S(1)}, f32[8,128]{1,0:T(8,128)S(1)}, u32[]{:S(2)}, u32[]{:S(2)}) collective-permute-start(f32[8,128]{1,0:T(8,128)S(1)} %convert_reduce_fusion.power), channel_id=1, source_target_pairs={{0,16},{16,0},{1,17},{17,1},{2,18},{18,2},{3,19},{19,3},{4,20},{20... | collective-permute-start | bytes 12296 | tf_op jit(solution)/shard_map/ppermute | solution.py:311
  132.6 0.8 collective-permute-done.3.other
  133.4 0.6 tile_phasor.1
  (3 shorter events, 0.1 us)
Async XLA Ops:
  6.6 10.3 %collective-permute-start = (bf16[512,512]{1,0:T(8,128)(2,1)S(1)}, bf16[512,512]{1,0:T(8,128)(2,1)S(1)}, u32[]{:S(2)}, u32[]{:S(2)}) collective-permute-start(bf16[512,512]{1,0:T(8,128)(2,1)S(1)} %get-tuple-element.10), channel_id=1, source_target_pairs={{0,16},{16,0},{1,17},{17,1},{2,18},{18,2},{3,19},{19,3},{4,20},{20... | collective-permute-start | bytes 1572872 | tf_op jit(solution)/shard_map/ppermute | solution.py:311
  68.7 7.8 %collective-permute-start.1 = (bf16[32,16,512]{2,1,0:T(8,128)(2,1)S(1)}, bf16[32,16,512]{2,1,0:T(8,128)(2,1)S(1)}, u32[]{:S(2)}, u32[]{:S(2)}) collective-permute-start(bf16[32,16,512]{2,1,0:T(8,128)(2,1)S(1)} %all_to_all.32.after.own), channel_id=1, source_target_pairs={{0,16},{16,0},{1,17},{17,1},{2,18},{18,2},{3,19},{19,3},{4,20},{20... | collective-permute-start | bytes 1572872 | tf_op jit(solution)/shard_map/ppermute | solution.py:311
  74.9 1.5 %copy-start = (bf16[1,1,2,512,512]{4,3,2,1,0:T(8,128)(2,1)S(1)}, bf16[1,1,2,512,512]{4,3,2,1,0:T(8,128)(2,1)}, u32[]{:S(2)}) copy-start(bf16[1,1,2,512,512]{4,3,2,1,0:T(8,128)(2,1)} %param.5) | copy-start | bytes 3145732
  74.9 1.5 %copy-start.1 = (bf16[1,1,2,512,512]{4,3,2,1,0:T(8,128)(2,1)S(1)}, bf16[1,1,2,512,512]{4,3,2,1,0:T(8,128)(2,1)}, u32[]{:S(2)}) copy-start(bf16[1,1,2,512,512]{4,3,2,1,0:T(8,128)(2,1)} %param.4) | copy-start | bytes 3145732
  80.0 3.8 %collective-permute-start.2 = (bf16[16,16,8,128]{3,2,1,0:T(8,128)(2,1)S(1)}, bf16[16,16,8,128]{3,2,1,0:T(8,128)(2,1)S(1)}, u32[]{:S(2)}, u32[]{:S(2)}) collective-permute-start(bf16[16,16,8,128]{3,2,1,0:T(8,128)(2,1)S(1)} %get-tuple-element.13), channel_id=1, source_target_pairs={{0,16},{16,0},{1,17},{17,1},{2,18},{18,2},{3,19},{19,3},{4,20},{20... | collective-permute-start | bytes 1572872 | tf_op jit(solution)/shard_map/ppermute | solution.py:311
  125.9 7.4 %collective-permute-start.3 = (f32[8,128]{1,0:T(8,128)S(1)}, f32[8,128]{1,0:T(8,128)S(1)}, u32[]{:S(2)}, u32[]{:S(2)}) collective-permute-start(f32[8,128]{1,0:T(8,128)S(1)} %convert_reduce_fusion.power), channel_id=1, source_target_pairs={{0,16},{16,0},{1,17},{17,1},{2,18},{18,2},{3,19},{19,3},{4,20},{20... | collective-permute-start | bytes 12296 | tf_op jit(solution)/shard_map/ppermute | solution.py:311

commit v6 on v5

--- a/solution.py
+++ b/solution.py
@@ -14,11 +14,20 @@
 WAVE = ("xl", "z")
 MIB = 1024 * 1024
 BLK = 128
+STEP = 256
 CHUNK = 16
 
 
 def dot(a, b):
     return jnp.dot(a, b, preferred_element_type=F32)
+
+
+def both(left, right):
+    rows = left.shape[1]
+    stacked = left.reshape(2 * rows, N)
+    p = dot(stacked, right[0])
+    q = dot(stacked, right[1])
+    return p[:rows], p[rows:], q[:rows], q[rows:]
 
 
 def chirp_into(scale, ar, ai):
@@ -44,8 +53,8 @@
     chirp_into(scale_ref[0], a.at[0], a.at[1])
 
 
-def back_kernel(scale_ref, core_ref, tgt_hbm, old_hbm, fld_hbm, keep, send, tgt, old, fld, a, z_s, sems):
-    blocks = [slice(r, r + BLK) for r in range(0, N, BLK)]
+def back_kernel(scale_ref, core_ref, tgt_hbm, old_hbm, fld_hbm, keep, send, tgt, old, fld, a, z_s, c_s, sems):
+    blocks = [slice(r, r + STEP) for r in range(0, N, STEP)]
     arrive = []
     for pairs in (((tgt_hbm, tgt), (old_hbm, old)), ((fld_hbm, fld),)):
         for rows in blocks:
@@ -61,16 +70,16 @@
         bi = tgt[1, rows].astype(F32)
         mr = old[0, rows].astype(F32)
         mi = old[1, rows].astype(F32)
-        cr = (br * mr + bi * mi).astype(BF)
-        ci = (bi * mr - br * mi).astype(BF)
-        z_s[0, rows] = (dot(cr, a[0]) + dot(ci, a[1])).astype(BF)
-        z_s[1, rows] = (dot(ci, a[0]) - dot(cr, a[1])).astype(BF)
+        c_s[0, rows] = (br * mr + bi * mi).astype(BF)
+        c_s[1, rows] = (bi * mr - br * mi).astype(BF)
+        rr, ir, ri, ii = both(c_s[:, rows], a)
+        z_s[0, rows] = (rr + ii).astype(BF)
+        z_s[1, rows] = (ir - ri).astype(BF)
     first = core_ref[0] == 0
     for i, rows in enumerate(blocks):
-        kr = a[0, rows]
-        ki = a[1, rows]
-        back_r = dot(kr, z_s[0]) + dot(ki, z_s[1])
-        back_i = dot(kr, z_s[1]) - dot(ki, z_s[0])
+        rr, ir, ri, ii = both(a[:, rows], z_s)
+        back_r = rr + ii
+        back_i = ri - ir
         arrive[2 * len(blocks) + i].wait()
         fr = fld[0, rows].astype(F32)
         fi = fld[1, rows].astype(F32)
@@ -186,7 +195,7 @@
 
 
 def call_back(scale, core, tgt, old, fld):
-    blocks = N // BLK
+    blocks = N // STEP
     return pl.pallas_call(
         back_kernel,
         out_shape=(
@@ -195,7 +204,7 @@
         ),
         in_specs=[SMEM, SMEM, HBM, HBM, HBM],
         out_specs=(VMEM,) * 2,
-        scratch_shapes=[pltpu.VMEM((2, N, N), BF)] * 5
+        scratch_shapes=[pltpu.VMEM((2, N, N), BF)] * 6
         + [
             pltpu.SemaphoreType.DMA((3 * blocks,)),
         ],

time: 134 us -> 134 us (level)
  no operation moved by 1% of the time
where the time goes in v6:
time: 134 us; the launch traced here: 133 us
  blocking collectives  93 us (69%)
  starting transfers between devices  23.9 us (18%)
  Pallas kernels  10.1 us (8%)
  waiting for transfers between devices  4.02 us (3%)
  between operations  1.41 us (1%)
    all_to_all x6, blocking collectives, exchange(): return lax.all_to_all(x, AXES, 0, 0, tiled=True, axis_index_groups=groups)  93 us
    ppermute x4, starting transfers between devices, swap_cores(): return lax.ppermute(x, 'c', [(0, 1), (1, 0)])  23.9 us
    pallas_call x1, Pallas kernels, call_back(): pl.pallas_call(back_kernel, out_shape=(jax.ShapeDtypeStruct((N, N), BF),...  4.46 us
    ppermute x4, waiting for transfers between devices, swap_cores(): return lax.ppermute(x, 'c', [(0, 1), (1, 0)])  4.02 us
    pallas_call x1, Pallas kernels, call_ahead(): pl.pallas_call(ahead_kernel, out_shape=(jax.ShapeDtypeStruct((2, 16, N),...  3.51 us
  transfers between devices with their start and end apart: 4, of which 4 were waited for; matrix products, arithmetic and copies ran while one was open for 0% of the time, Pallas kernels for 1%

profile of v6, /device:TPU:1, one launch (start us, length us, event | category | flops | bytes accessed | tf_op | source)
XLA Modules:
  0.0 133.1 jit_solution(17681923338907702831)
XLA Ops:
  1.3 4.5 %back_margin.1 = (bf16[512,512]{1,0:T(8,128)(2,1)S(1)}, bf16[512,512]{1,0:T(8,128)(2,1)S(1)}) custom-call(f32[1]{0:T(128)S(6)} %copy.6.scale_ref, s32[1]{0:T(128)} %bitcast.core_ref, bf16[2,512,512]{2,1,0:T(8,128)(2,1)} %bitcast.5, bf16[2,512,512]{2,1,0:T(8,128)(2,1)} %old_hbm.1, bf16[2,512,512]{2,1,0:T(8,128)(2,1)} %bitcast.8), custom_call_target="tpu_custom_call" | custom-call | tf_op jit(solution)/shard_map/back_margin/pallas_call | solution.py:199
  5.7 8.8 %collective-permute-start = (bf16[512,512]{1,0:T(8,128)(2,1)S(1)}, bf16[512,512]{1,0:T(8,128)(2,1)S(1)}, u32[]{:S(2)}, u32[]{:S(2)}) collective-permute-start(bf16[512,512]{1,0:T(8,128)(2,1)S(1)} %get-tuple-element.10), channel_id=1, source_target_pairs={{0,16},{16,0},{1,17},{17,1},{2,18},{18,2},{3,19},{19,3},{4,20},{20... | collective-permute-start | bytes 1572872 | tf_op jit(solution)/shard_map/ppermute | solution.py:320
  14.5 1.5 %collective-permute-done = bf16[512,512]{1,0:T(8,128)(2,1)S(1)} collective-permute-done((bf16[512,512]{1,0:T(8,128)(2,1)S(1)}, bf16[512,512]{1,0:T(8,128)(2,1)S(1)}, u32[]{:S(2)}, u32[]{:S(2)}) %collective-permute-start) | collective-permute-done | bytes 524320 | tf_op jit(solution)/shard_map/ppermute | solution.py:320
  16.1 0.1 add_convert_fusion.1
  16.2 20.0 %all_to_all.30 = bf16[32,16,512]{2,1,0:T(8,128)(2,1)S(1)} all-to-all(bf16[32,16,512]{2,1,0:T(8,128)(2,1)S(1)} %bitcast.10), channel_id=1, replica_groups={{0,8,32,40,64,72,96,104,128,136,160,168,192,200,224,232,256,264,288,296..., dimensions={0} | all-to-all | bytes 1048576 | tf_op jit(solution)/shard_map/all_to_all | solution.py:308
  36.2 0.1 reduce_sum.45
  36.3 14.5 %all_to_all.31 = bf16[8,16,512]{2,1,0:T(8,128)(2,1)S(1)} all-to-all(bf16[8,16,512]{2,1,0:T(8,128)(2,1)S(1)} %broadcast_in_dim.6), channel_id=1, replica_groups={{0,1,2,3,4,5,6,7},{8,9,10,11,12,13,14,15},{32,33,34,35,36,37,38,39},{40..., dimensions={0} | all-to-all | bytes 262144 | tf_op jit(solution)/shard_map/all_to_all | solution.py:308
  50.9 0.1 broadcast_in_dim.7
  50.9 16.9 %all_to_all.32.after.own = bf16[32,16,512]{2,1,0:T(8,128)(2,1)S(1)} all-to-all(bf16[32,16,512]{2,1,0:T(8,128)(2,1)S(1)} %broadcast_in_dim.7), channel_id=1, replica_groups={{0,8,32,40,64,72,96,104,128,136,160,168,192,200,224,232,256,264,288,296..., dimensions={0} | all-to-all | bytes 1048576 | tf_op jit(solution)/shard_map/all_to_all | solution.py:308
  67.8 6.2 %collective-permute-start.1 = (bf16[32,16,512]{2,1,0:T(8,128)(2,1)S(1)}, bf16[32,16,512]{2,1,0:T(8,128)(2,1)S(1)}, u32[]{:S(2)}, u32[]{:S(2)}) collective-permute-start(bf16[32,16,512]{2,1,0:T(8,128)(2,1)S(1)} %all_to_all.32.after.own), channel_id=1, source_target_pairs={{0,16},{16,0},{1,17},{17,1},{2,18},{18,2},{3,19},{19,3},{4,20},{20... | collective-permute-start | bytes 1572872 | tf_op jit(solution)/shard_map/ppermute | solution.py:320
  74.1 0.0 copy-start
  74.1 0.0 copy-start.1
  74.1 0.3 chirp.1.a_ref
  74.4 1.2 collective-permute-done.1.other
  75.6 0.0 copy-done
  75.6 0.0 copy-done.1
  75.6 3.5 %ahead_margin.1 = (bf16[2,16,512]{2,1,0:T(8,128)(2,1)}, bf16[2,512,512]{2,1,0:T(8,128)(2,1)S(1)}, bf16[16,16,8,128]{3,2,1,0:T(8,128)(2,1)S(1)}) custom-call(s32[1]{0:T(128)} %bitcast.core_ref, s32[1]{0:T(128)} %bitcast.1.mode_ref, bf16[32,16,512]{2,1,0:T(8,128)(2,1)S(1)} %all_to_all.32.after.own, bf16[32,16,512]{2,1,0:T(8,128)(2,1)S(1)} %collective-permute-done.1.other, ...), custom_call_target="tpu_custom_call" | custom-call | tf_op jit(solution)/shard_map/ahead_margin/pallas_call | solution.py:217
  79.1 2.2 %collective-permute-start.2 = (bf16[16,16,8,128]{3,2,1,0:T(8,128)(2,1)S(1)}, bf16[16,16,8,128]{3,2,1,0:T(8,128)(2,1)S(1)}, u32[]{:S(2)}, u32[]{:S(2)}) collective-permute-start(bf16[16,16,8,128]{3,2,1,0:T(8,128)(2,1)S(1)} %get-tuple-element.13), channel_id=1, source_target_pairs={{0,16},{16,0},{1,17},{17,1},{2,18},{18,2},{3,19},{19,3},{4,20},{20... | collective-permute-start | bytes 1572872 | tf_op jit(solution)/shard_map/ppermute | solution.py:320
  81.4 1.0 keep_margin.1
  82.4 0.6 collective-permute-done.2
  82.9 0.2 add_convert_fusion
  83.1 13.2 %all_to_all.33 = bf16[16,16,8,128]{3,2,1,0:T(8,128)(2,1)S(1)} all-to-all(bf16[16,16,8,128]{3,2,1,0:T(8,128)(2,1)S(1)} %add_convert_fusion), channel_id=1, replica_groups={{0,32,64,96,128,160,192,224,256,288,320,352,384,416,448,480},{1,33,65,9..., dimensions={0} | all-to-all | bytes 1048576 | tf_op jit(solution)/shard_map/all_to_all | solution.py:308
  96.3 0.1 reduce_sum.47
  96.3 0.1 broadcast_in_dim.8
  96.4 17.1 %all_to_all.34.parts = bf16[16,16,8,128]{3,2,1,0:T(8,128)(2,1)S(1)} all-to-all(bf16[16,16,8,128]{3,2,1,0:T(8,128)(2,1)S(1)} %broadcast_in_dim.8), channel_id=1, replica_groups={{16,48,80,112,144,176,208,240,272,304,336,368,400,432,464,496},{17,49,8..., dimensions={0} | all-to-all | bytes 1048576 | tf_op jit(solution)/shard_map/all_to_all | solution.py:308
  113.5 0.2 tile_power.1
  113.8 11.3 %all_to_all.35.arrived = bf16[16,16,128]{2,1,0:T(8,128)(2,1)S(1)} all-to-all(bf16[16,16,128]{2,1,0:T(8,128)(2,1)S(1)} %get-tuple-element.15), channel_id=1, replica_groups={{0,32,64,96,128,160,192,224,256,288,320,352,384,416,448,480},{1,33,65,9..., dimensions={0} | all-to-all | bytes 131072 | tf_op jit(solution)/shard_map/all_to_all | solution.py:308
  125.1 6.6 %collective-permute-start.3 = (f32[8,128]{1,0:T(8,128)S(1)}, f32[8,128]{1,0:T(8,128)S(1)}, u32[]{:S(2)}, u32[]{:S(2)}) collective-permute-start(f32[8,128]{1,0:T(8,128)S(1)} %convert_reduce_fusion.power), channel_id=1, source_target_pairs={{0,16},{16,0},{1,17},{17,1},{2,18},{18,2},{3,19},{19,3},{4,20},{20... | collective-permute-start | bytes 12296 | tf_op jit(solution)/shard_map/ppermute | solution.py:320
  131.7 0.8 collective-permute-done.3.other
  132.5 0.6 tile_phasor.1
  (3 shorter events, 0.1 us)
Async XLA Ops:
  5.7 10.3 %collective-permute-start = (bf16[512,512]{1,0:T(8,128)(2,1)S(1)}, bf16[512,512]{1,0:T(8,128)(2,1)S(1)}, u32[]{:S(2)}, u32[]{:S(2)}) collective-permute-start(bf16[512,512]{1,0:T(8,128)(2,1)S(1)} %get-tuple-element.10), channel_id=1, source_target_pairs={{0,16},{16,0},{1,17},{17,1},{2,18},{18,2},{3,19},{19,3},{4,20},{20... | collective-permute-start | bytes 1572872 | tf_op jit(solution)/shard_map/ppermute | solution.py:320
  67.8 7.8 %collective-permute-start.1 = (bf16[32,16,512]{2,1,0:T(8,128)(2,1)S(1)}, bf16[32,16,512]{2,1,0:T(8,128)(2,1)S(1)}, u32[]{:S(2)}, u32[]{:S(2)}) collective-permute-start(bf16[32,16,512]{2,1,0:T(8,128)(2,1)S(1)} %all_to_all.32.after.own), channel_id=1, source_target_pairs={{0,16},{16,0},{1,17},{17,1},{2,18},{18,2},{3,19},{19,3},{4,20},{20... | collective-permute-start | bytes 1572872 | tf_op jit(solution)/shard_map/ppermute | solution.py:320
  74.1 1.5 %copy-start = (bf16[1,1,2,512,512]{4,3,2,1,0:T(8,128)(2,1)S(1)}, bf16[1,1,2,512,512]{4,3,2,1,0:T(8,128)(2,1)}, u32[]{:S(2)}) copy-start(bf16[1,1,2,512,512]{4,3,2,1,0:T(8,128)(2,1)} %param.5) | copy-start | bytes 3145732
  74.1 1.5 %copy-start.1 = (bf16[1,1,2,512,512]{4,3,2,1,0:T(8,128)(2,1)S(1)}, bf16[1,1,2,512,512]{4,3,2,1,0:T(8,128)(2,1)}, u32[]{:S(2)}) copy-start(bf16[1,1,2,512,512]{4,3,2,1,0:T(8,128)(2,1)} %param.4) | copy-start | bytes 3145732
  79.1 3.8 %collective-permute-start.2 = (bf16[16,16,8,128]{3,2,1,0:T(8,128)(2,1)S(1)}, bf16[16,16,8,128]{3,2,1,0:T(8,128)(2,1)S(1)}, u32[]{:S(2)}, u32[]{:S(2)}) collective-permute-start(bf16[16,16,8,128]{3,2,1,0:T(8,128)(2,1)S(1)} %get-tuple-element.13), channel_id=1, source_target_pairs={{0,16},{16,0},{1,17},{17,1},{2,18},{18,2},{3,19},{19,3},{4,20},{20... | collective-permute-start | bytes 1572872 | tf_op jit(solution)/shard_map/ppermute | solution.py:320
  125.1 7.4 %collective-permute-start.3 = (f32[8,128]{1,0:T(8,128)S(1)}, f32[8,128]{1,0:T(8,128)S(1)}, u32[]{:S(2)}, u32[]{:S(2)}) collective-permute-start(f32[8,128]{1,0:T(8,128)S(1)} %convert_reduce_fusion.power), channel_id=1, source_target_pairs={{0,16},{16,0},{1,17},{17,1},{2,18},{18,2},{3,19},{19,3},{4,20},{20... | collective-permute-start | bytes 12296 | tf_op jit(solution)/shard_map/ppermute | solution.py:320

commit v7 on v6

--- a/solution.py
+++ b/solution.py
@@ -111,7 +111,7 @@
                 out[jnp.where(by_mode, q, w), jnp.where(by_mode, w, q)] = tile.astype(out.dtype)
 
 
-def ahead_kernel(core_ref, mode_ref, own, other, a_ref, tgt, fld, mask_out, z_s, send, mask):
+def ahead_kernel(core_ref, mode_ref, own, other, a_ref, tgt, fld, term, mine, z_s, send):
     first = core_ref[0] == 0
     total = jnp.zeros((CHUNK, N), F32)
     for r in range(N // CHUNK):
@@ -128,8 +128,6 @@
         b = b * factor
         mr = jnp.where(first, a, b).astype(BF)
         mi = jnp.where(first, b, a).astype(BF)
-        mask[0, rows] = mr
-        mask[1, rows] = mi
         mr = mr.astype(F32)
         mi = mi.astype(F32)
         fr = fld[0, rows].astype(F32)
@@ -138,9 +136,9 @@
         gi = (fr * mi + fi * mr).astype(BF)
         z_s[0, rows] = (dot(gr, a_ref[0]) - dot(gi, a_ref[1])).astype(BF)
         z_s[1, rows] = (dot(gi, a_ref[0]) + dot(gr, a_ref[1])).astype(BF)
-    start = pl.multiple_of(mode_ref[0] * 16, 16)
-    mask_out[0] = mask[0, pl.ds(start, 16)]
-    mask_out[1] = mask[1, pl.ds(start, 16)]
+    term[...] = jnp.full((8, 128), bias, F32)
+    mine[0] = own[mode_ref[0]]
+    mine[1] = other[mode_ref[0]]
     ahead_rows(1 - core_ref[0], core_ref[0] != 0, a_ref, z_s, tgt, send)
 
 
@@ -162,8 +160,15 @@
         message[k] = mine
 
 
-def phasor_kernel(core_ref, tiles, arrived, power, other, out, full):
+def phasor_kernel(core_ref, tiles, arrived, power, other, mine, term, mask_one, out, full):
     first = core_ref[0] == 0
+    a = mine[0].astype(F32)
+    b = mine[1].astype(F32)
+    factor = lax.rsqrt(a * a + b * b + term[:1, :1])
+    a = a * factor
+    b = b * factor
+    mask_one[0] = jnp.where(first, a, b).astype(BF)
+    mask_one[1] = jnp.where(first, b, a).astype(BF)
     bias = jnp.sum(power[...] + other[...], 0, keepdims=True) / (4 * N * N) + 1e-06
     for half in range(2):
         for col in range(4):
@@ -217,13 +222,13 @@
     return pl.pallas_call(
         ahead_kernel,
         out_shape=(
-            jax.ShapeDtypeStruct((2, 16, N), BF),
+            jax.ShapeDtypeStruct((8, 128), F32),
+            jax.ShapeDtypeStruct((2, CHUNK, N), BF),
             jax.ShapeDtypeStruct((2, N, N), BF),
             jax.ShapeDtypeStruct((16, 16, 8, 128), BF),
         ),
         in_specs=[SMEM, SMEM] + [VMEM] * 5,
-        out_specs=(VMEM,) * 3,
-        scratch_shapes=[pltpu.VMEM((2, N, N), BF)],
+        out_specs=(VMEM,) * 4,
         compiler_params=pltpu.CompilerParams(vmem_limit_bytes=16 * MIB),
         name="ahead_margin",
     )(core, mode, own, other, a, tgt, fld)
@@ -252,16 +257,16 @@
     )(mode, parts)
 
 
-def call_phasor(core, tiles, arrived, power, other):
+def call_phasor(core, *arrays):
     return pl.pallas_call(
         phasor_kernel,
-        out_shape=jax.ShapeDtypeStruct((2, 16, N), BF),
-        in_specs=[SMEM] + [VMEM] * 4,
-        out_specs=VMEM,
+        out_shape=(jax.ShapeDtypeStruct((2, 16, N), BF),) * 2,
+        in_specs=[SMEM] + [VMEM] * 6,
+        out_specs=(VMEM, VMEM),
         scratch_shapes=[pltpu.VMEM((2, 16, N), F32)],
         compiler_params=pltpu.CompilerParams(vmem_limit_bytes=8 * MIB),
         name="tile_phasor",
-    )(core, tiles, arrived, power, other)
+    )(core, *arrays)
 
 
 def device(y, xh, c, xl, z):
@@ -332,7 +337,7 @@
     own = spread(part, WIDE)
     other = swap_cores(own)
     a = call_chirp(scales, own)
-    mask_one, middle, send = call_ahead(core, mode, own, other, a, tgt, fld)
+    term, mine, middle, send = call_ahead(core, mode, own, other, a, tgt, fld)
     came = swap_cores(send)
     keep = call_keep(core, a, middle, tgt)
     half = (keep + came.astype(F32)).astype(BF)
@@ -340,7 +345,7 @@
     tiles, message = call_power(mode, spread(part, RING_B))
     arrived = exchange(message, RING_A)
     power = jnp.sum(arrived[:, 8:].astype(F32), 0)
-    return mask_one, call_phasor(core, tiles, arrived, power, swap_cores(power))
+    return call_phasor(core, tiles, arrived, power, swap_cores(power), mine, term)
 
 
 def solution(mesh):

time: 134 us -> 133 us (level)
  no operation moved by 1% of the time
where the time goes in v7:
time: 133 us
  blocking collectives  93 us (70%)
  starting transfers between devices  23.9 us (18%)
  Pallas kernels  9.53 us (7%)
  waiting for transfers between devices  4.01 us (3%)
  between operations  1.41 us (1%)
    all_to_all x6, blocking collectives, exchange(): return lax.all_to_all(x, AXES, 0, 0, tiled=True, axis_index_groups=groups)  93 us
    ppermute x4, starting transfers between devices, swap_cores(): return lax.ppermute(x, 'c', [(0, 1), (1, 0)])  23.9 us
    pallas_call x1, Pallas kernels, call_back(): pl.pallas_call(back_kernel, out_shape=(jax.ShapeDtypeStruct((N, N), BF),...  4.46 us
    ppermute x4, waiting for transfers between devices, swap_cores(): return lax.ppermute(x, 'c', [(0, 1), (1, 0)])  4.01 us
    pallas_call x1, Pallas kernels, call_ahead(): pl.pallas_call(ahead_kernel, out_shape=(jax.ShapeDtypeStruct((8, 128), F3...  2.87 us
  transfers between devices with their start and end apart: 4, of which 4 were waited for; matrix products, arithmetic and copies ran while one was open for 0% of the time, Pallas kernels for 1%

profile of v7, /device:TPU:1, one launch (start us, length us, event | category | flops | bytes accessed | tf_op | source)
XLA Modules:
  0.0 132.5 jit_solution(2459269603158183559)
XLA Ops:
  1.3 4.5 %back_margin.1 = (bf16[512,512]{1,0:T(8,128)(2,1)S(1)}, bf16[512,512]{1,0:T(8,128)(2,1)S(1)}) custom-call(f32[1]{0:T(128)S(6)} %copy.6.scale_ref, s32[1]{0:T(128)} %bitcast.core_ref, bf16[2,512,512]{2,1,0:T(8,128)(2,1)} %bitcast.5, bf16[2,512,512]{2,1,0:T(8,128)(2,1)} %old_hbm.1, bf16[2,512,512]{2,1,0:T(8,128)(2,1)} %bitcast.8), custom_call_target="tpu_custom_call" | custom-call | tf_op jit(solution)/shard_map/back_margin/pallas_call | solution.py:204
  5.7 8.8 %collective-permute-start = (bf16[512,512]{1,0:T(8,128)(2,1)S(1)}, bf16[512,512]{1,0:T(8,128)(2,1)S(1)}, u32[]{:S(2)}, u32[]{:S(2)}) collective-permute-start(bf16[512,512]{1,0:T(8,128)(2,1)S(1)} %get-tuple-element.11), channel_id=1, source_target_pairs={{0,16},{16,0},{1,17},{17,1},{2,18},{18,2},{3,19},{19,3},{4,20},{20... | collective-permute-start | bytes 1572872 | tf_op jit(solution)/shard_map/ppermute | solution.py:325
  14.5 1.5 %collective-permute-done = bf16[512,512]{1,0:T(8,128)(2,1)S(1)} collective-permute-done((bf16[512,512]{1,0:T(8,128)(2,1)S(1)}, bf16[512,512]{1,0:T(8,128)(2,1)S(1)}, u32[]{:S(2)}, u32[]{:S(2)}) %collective-permute-start) | collective-permute-done | bytes 524320 | tf_op jit(solution)/shard_map/ppermute | solution.py:325
  16.1 0.1 add_convert_fusion.1
  16.2 20.0 %all_to_all.30 = bf16[32,16,512]{2,1,0:T(8,128)(2,1)S(1)} all-to-all(bf16[32,16,512]{2,1,0:T(8,128)(2,1)S(1)} %bitcast.10), channel_id=1, replica_groups={{0,8,32,40,64,72,96,104,128,136,160,168,192,200,224,232,256,264,288,296..., dimensions={0} | all-to-all | bytes 1048576 | tf_op jit(solution)/shard_map/all_to_all | solution.py:313
  36.2 0.1 reduce_sum.45
  36.3 14.5 %all_to_all.31 = bf16[8,16,512]{2,1,0:T(8,128)(2,1)S(1)} all-to-all(bf16[8,16,512]{2,1,0:T(8,128)(2,1)S(1)} %broadcast_in_dim.6), channel_id=1, replica_groups={{0,1,2,3,4,5,6,7},{8,9,10,11,12,13,14,15},{32,33,34,35,36,37,38,39},{40..., dimensions={0} | all-to-all | bytes 262144 | tf_op jit(solution)/shard_map/all_to_all | solution.py:313
  50.9 0.1 broadcast_in_dim.7
  50.9 16.9 %all_to_all.32.after.own = bf16[32,16,512]{2,1,0:T(8,128)(2,1)S(1)} all-to-all(bf16[32,16,512]{2,1,0:T(8,128)(2,1)S(1)} %broadcast_in_dim.7), channel_id=1, replica_groups={{0,8,32,40,64,72,96,104,128,136,160,168,192,200,224,232,256,264,288,296..., dimensions={0} | all-to-all | bytes 1048576 | tf_op jit(solution)/shard_map/all_to_all | solution.py:313
  67.8 6.2 %collective-permute-start.1 = (bf16[32,16,512]{2,1,0:T(8,128)(2,1)S(1)}, bf16[32,16,512]{2,1,0:T(8,128)(2,1)S(1)}, u32[]{:S(2)}, u32[]{:S(2)}) collective-permute-start(bf16[32,16,512]{2,1,0:T(8,128)(2,1)S(1)} %all_to_all.32.after.own), channel_id=1, source_target_pairs={{0,16},{16,0},{1,17},{17,1},{2,18},{18,2},{3,19},{19,3},{4,20},{20... | collective-permute-start | bytes 1572872 | tf_op jit(solution)/shard_map/ppermute | solution.py:325
  74.1 0.0 copy-start
  74.1 0.0 copy-start.1
  74.1 0.3 chirp.1.a_ref
  74.4 1.2 collective-permute-done.1.other
  75.6 0.0 copy-done
  75.6 0.0 copy-done.1
  75.6 2.9 %ahead_margin.1 = (f32[8,128]{1,0:T(8,128)S(1)}, bf16[2,16,512]{2,1,0:T(8,128)(2,1)S(1)}, bf16[2,512,512]{2,1,0:T(8,128)(2,1)S(1)}, bf16[16,16,8,128]{3,2,1,0:T(8,128)(2,1)S(1)}) custom-call(s32[1]{0:T(128)} %bitcast.core_ref, s32[1]{0:T(128)} %bitcast.1.mode_ref, bf16[32,16,512]{2,1,0:T(8,128)(2,1)S(1)} %all_to_all.32.after.own, ...), custom_call_target="tpu_custom_call" | custom-call | tf_op jit(solution)/shard_map/ahead_margin/pallas_call | solution.py:222
  78.5 2.2 %collective-permute-start.2 = (bf16[16,16,8,128]{3,2,1,0:T(8,128)(2,1)S(1)}, bf16[16,16,8,128]{3,2,1,0:T(8,128)(2,1)S(1)}, u32[]{:S(2)}, u32[]{:S(2)}) collective-permute-start(bf16[16,16,8,128]{3,2,1,0:T(8,128)(2,1)S(1)} %get-tuple-element.13), channel_id=1, source_target_pairs={{0,16},{16,0},{1,17},{17,1},{2,18},{18,2},{3,19},{19,3},{4,20},{20... | collective-permute-start | bytes 1572872 | tf_op jit(solution)/shard_map/ppermute | solution.py:325
  80.8 1.0 keep_margin.1
  81.8 0.5 collective-permute-done.2
  82.3 0.1 add_convert_fusion
  82.4 13.2 %all_to_all.33 = bf16[16,16,8,128]{3,2,1,0:T(8,128)(2,1)S(1)} all-to-all(bf16[16,16,8,128]{3,2,1,0:T(8,128)(2,1)S(1)} %add_convert_fusion), channel_id=1, replica_groups={{0,32,64,96,128,160,192,224,256,288,320,352,384,416,448,480},{1,33,65,9..., dimensions={0} | all-to-all | bytes 1048576 | tf_op jit(solution)/shard_map/all_to_all | solution.py:313
  95.6 0.1 reduce_sum.47
  95.7 0.1 broadcast_in_dim.8
  95.8 17.1 %all_to_all.34.parts = bf16[16,16,8,128]{3,2,1,0:T(8,128)(2,1)S(1)} all-to-all(bf16[16,16,8,128]{3,2,1,0:T(8,128)(2,1)S(1)} %broadcast_in_dim.8), channel_id=1, replica_groups={{16,48,80,112,144,176,208,240,272,304,336,368,400,432,464,496},{17,49,8..., dimensions={0} | all-to-all | bytes 1048576 | tf_op jit(solution)/shard_map/all_to_all | solution.py:313
  112.9 0.2 tile_power.1
  113.1 11.3 %all_to_all.35.arrived = bf16[16,16,128]{2,1,0:T(8,128)(2,1)S(1)} all-to-all(bf16[16,16,128]{2,1,0:T(8,128)(2,1)S(1)} %get-tuple-element.15), channel_id=1, replica_groups={{0,32,64,96,128,160,192,224,256,288,320,352,384,416,448,480},{1,33,65,9..., dimensions={0} | all-to-all | bytes 131072 | tf_op jit(solution)/shard_map/all_to_all | solution.py:313
  124.4 6.6 %collective-permute-start.3 = (f32[8,128]{1,0:T(8,128)S(1)}, f32[8,128]{1,0:T(8,128)S(1)}, u32[]{:S(2)}, u32[]{:S(2)}) collective-permute-start(f32[8,128]{1,0:T(8,128)S(1)} %convert_reduce_fusion.power), channel_id=1, source_target_pairs={{0,16},{16,0},{1,17},{17,1},{2,18},{18,2},{3,19},{19,3},{4,20},{20... | collective-permute-start | bytes 12296 | tf_op jit(solution)/shard_map/ppermute | solution.py:325
  131.1 0.8 collective-permute-done.3.other
  131.9 0.7 tile_phasor.1
  (3 shorter events, 0.1 us)
Async XLA Ops:
  5.7 10.3 %collective-permute-start = (bf16[512,512]{1,0:T(8,128)(2,1)S(1)}, bf16[512,512]{1,0:T(8,128)(2,1)S(1)}, u32[]{:S(2)}, u32[]{:S(2)}) collective-permute-start(bf16[512,512]{1,0:T(8,128)(2,1)S(1)} %get-tuple-element.11), channel_id=1, source_target_pairs={{0,16},{16,0},{1,17},{17,1},{2,18},{18,2},{3,19},{19,3},{4,20},{20... | collective-permute-start | bytes 1572872 | tf_op jit(solution)/shard_map/ppermute | solution.py:325
  67.8 7.8 %collective-permute-start.1 = (bf16[32,16,512]{2,1,0:T(8,128)(2,1)S(1)}, bf16[32,16,512]{2,1,0:T(8,128)(2,1)S(1)}, u32[]{:S(2)}, u32[]{:S(2)}) collective-permute-start(bf16[32,16,512]{2,1,0:T(8,128)(2,1)S(1)} %all_to_all.32.after.own), channel_id=1, source_target_pairs={{0,16},{16,0},{1,17},{17,1},{2,18},{18,2},{3,19},{19,3},{4,20},{20... | collective-permute-start | bytes 1572872 | tf_op jit(solution)/shard_map/ppermute | solution.py:325
  74.1 1.5 %copy-start = (bf16[1,1,2,512,512]{4,3,2,1,0:T(8,128)(2,1)S(1)}, bf16[1,1,2,512,512]{4,3,2,1,0:T(8,128)(2,1)}, u32[]{:S(2)}) copy-start(bf16[1,1,2,512,512]{4,3,2,1,0:T(8,128)(2,1)} %param.5) | copy-start | bytes 3145732
  74.1 1.5 %copy-start.1 = (bf16[1,1,2,512,512]{4,3,2,1,0:T(8,128)(2,1)S(1)}, bf16[1,1,2,512,512]{4,3,2,1,0:T(8,128)(2,1)}, u32[]{:S(2)}) copy-start(bf16[1,1,2,512,512]{4,3,2,1,0:T(8,128)(2,1)} %param.4) | copy-start | bytes 3145732
  78.5 3.8 %collective-permute-start.2 = (bf16[16,16,8,128]{3,2,1,0:T(8,128)(2,1)S(1)}, bf16[16,16,8,128]{3,2,1,0:T(8,128)(2,1)S(1)}, u32[]{:S(2)}, u32[]{:S(2)}) collective-permute-start(bf16[16,16,8,128]{3,2,1,0:T(8,128)(2,1)S(1)} %get-tuple-element.13), channel_id=1, source_target_pairs={{0,16},{16,0},{1,17},{17,1},{2,18},{18,2},{3,19},{19,3},{4,20},{20... | collective-permute-start | bytes 1572872 | tf_op jit(solution)/shard_map/ppermute | solution.py:325
  124.4 7.4 %collective-permute-start.3 = (f32[8,128]{1,0:T(8,128)S(1)}, f32[8,128]{1,0:T(8,128)S(1)}, u32[]{:S(2)}, u32[]{:S(2)}) collective-permute-start(f32[8,128]{1,0:T(8,128)S(1)} %convert_reduce_fusion.power), channel_id=1, source_target_pairs={{0,16},{16,0},{1,17},{17,1},{2,18},{18,2},{3,19},{19,3},{4,20},{20... | collective-permute-start | bytes 12296 | tf_op jit(solution)/shard_map/ppermute | solution.py:325

commit v8 on v7

--- a/solution.py
+++ b/solution.py
@@ -60,12 +60,16 @@
         for rows in blocks:
             for src, dst in pairs:
                 arrive.append(pltpu.make_async_copy(src.at[:, rows], dst.at[:, rows], sems.at[len(arrive)]))
-    for copy in arrive:
+    late = 2 * len(blocks)
+    for copy in arrive[:late]:
         copy.start()
     chirp_into(scale_ref[0], a.at[0], a.at[1])
     for i, rows in enumerate(blocks):
         arrive[2 * i].wait()
         arrive[2 * i + 1].wait()
+        if i == 0:
+            for copy in arrive[late:]:
+                copy.start()
         br = tgt[0, rows].astype(F32)
         bi = tgt[1, rows].astype(F32)
         mr = old[0, rows].astype(F32)
@@ -76,15 +80,15 @@
         z_s[0, rows] = (rr + ii).astype(BF)
         z_s[1, rows] = (ir - ri).astype(BF)
     first = core_ref[0] == 0
+    rr, ir, ri, ii = both(a[...], z_s)
+    back_r = rr + ii
+    back_i = ri - ir
     for i, rows in enumerate(blocks):
-        rr, ir, ri, ii = both(a[:, rows], z_s)
-        back_r = rr + ii
-        back_i = ri - ir
-        arrive[2 * len(blocks) + i].wait()
+        arrive[late + i].wait()
         fr = fld[0, rows].astype(F32)
         fi = fld[1, rows].astype(F32)
-        term_r = back_r * fr + back_i * fi
-        term_i = back_i * fr - back_r * fi
+        term_r = back_r[rows] * fr + back_i[rows] * fi
+        term_i = back_i[rows] * fr - back_r[rows] * fi
         send[rows] = jnp.where(first, term_i, term_r).astype(BF)
         keep[rows] = jnp.where(first, term_r, term_i).astype(BF)
 

time: 133 us -> 133 us (level)
  no operation moved by 1% of the time
where the time goes in v8:
time: 133 us; the launch traced here: 132 us
  blocking collectives  93 us (70%)
  starting transfers between devices  23.9 us (18%)
  Pallas kernels  9.24 us (7%)
  waiting for transfers between devices  4.01 us (3%)
  between operations  1.41 us (1%)
    all_to_all x6, blocking collectives, exchange(): return lax.all_to_all(x, AXES, 0, 0, tiled=True, axis_index_groups=groups)  93 us
    ppermute x4, starting transfers between devices, swap_cores(): return lax.ppermute(x, 'c', [(0, 1), (1, 0)])  23.9 us
    pallas_call x1, Pallas kernels, call_back(): pl.pallas_call(back_kernel, out_shape=(jax.ShapeDtypeStruct((N, N), BF),...  4.19 us
    ppermute x4, waiting for transfers between devices, swap_cores(): return lax.ppermute(x, 'c', [(0, 1), (1, 0)])  4.01 us
    pallas_call x1, Pallas kernels, call_ahead(): pl.pallas_call(ahead_kernel, out_shape=(jax.ShapeDtypeStruct((8, 128), F3...  2.86 us
  transfers between devices with their start and end apart: 4, of which 4 were waited for; matrix products, arithmetic and copies ran while one was open for 0% of the time, Pallas kernels for 1%

profile of v8, /device:TPU:1, one launch (start us, length us, event | category | flops | bytes accessed | tf_op | source)
XLA Modules:
  0.0 132.3 jit_solution(13751633990177649624)
XLA Ops:
  1.3 4.2 %back_margin.1 = (bf16[512,512]{1,0:T(8,128)(2,1)S(1)}, bf16[512,512]{1,0:T(8,128)(2,1)S(1)}) custom-call(f32[1]{0:T(128)S(6)} %copy.6.scale_ref, s32[1]{0:T(128)} %bitcast.core_ref, bf16[2,512,512]{2,1,0:T(8,128)(2,1)} %bitcast.5, bf16[2,512,512]{2,1,0:T(8,128)(2,1)} %old_hbm.1, bf16[2,512,512]{2,1,0:T(8,128)(2,1)} %bitcast.8), custom_call_target="tpu_custom_call" | custom-call | tf_op jit(solution)/shard_map/back_margin/pallas_call | solution.py:208
  5.5 8.8 %collective-permute-start = (bf16[512,512]{1,0:T(8,128)(2,1)S(1)}, bf16[512,512]{1,0:T(8,128)(2,1)S(1)}, u32[]{:S(2)}, u32[]{:S(2)}) collective-permute-start(bf16[512,512]{1,0:T(8,128)(2,1)S(1)} %get-tuple-element.11), channel_id=1, source_target_pairs={{0,16},{16,0},{1,17},{17,1},{2,18},{18,2},{3,19},{19,3},{4,20},{20... | collective-permute-start | bytes 1572872 | tf_op jit(solution)/shard_map/ppermute | solution.py:329
  14.3 1.5 %collective-permute-done = bf16[512,512]{1,0:T(8,128)(2,1)S(1)} collective-permute-done((bf16[512,512]{1,0:T(8,128)(2,1)S(1)}, bf16[512,512]{1,0:T(8,128)(2,1)S(1)}, u32[]{:S(2)}, u32[]{:S(2)}) %collective-permute-start) | collective-permute-done | bytes 524320 | tf_op jit(solution)/shard_map/ppermute | solution.py:329
  15.8 0.1 add_convert_fusion.1
  15.9 20.0 %all_to_all.30 = bf16[32,16,512]{2,1,0:T(8,128)(2,1)S(1)} all-to-all(bf16[32,16,512]{2,1,0:T(8,128)(2,1)S(1)} %bitcast.10), channel_id=1, replica_groups={{0,8,32,40,64,72,96,104,128,136,160,168,192,200,224,232,256,264,288,296..., dimensions={0} | all-to-all | bytes 1048576 | tf_op jit(solution)/shard_map/all_to_all | solution.py:317
  35.9 0.1 reduce_sum.45
  36.0 14.5 %all_to_all.31 = bf16[8,16,512]{2,1,0:T(8,128)(2,1)S(1)} all-to-all(bf16[8,16,512]{2,1,0:T(8,128)(2,1)S(1)} %broadcast_in_dim.6), channel_id=1, replica_groups={{0,1,2,3,4,5,6,7},{8,9,10,11,12,13,14,15},{32,33,34,35,36,37,38,39},{40..., dimensions={0} | all-to-all | bytes 262144 | tf_op jit(solution)/shard_map/all_to_all | solution.py:317
  50.6 0.1 broadcast_in_dim.7
  50.7 16.9 %all_to_all.32.after.own = bf16[32,16,512]{2,1,0:T(8,128)(2,1)S(1)} all-to-all(bf16[32,16,512]{2,1,0:T(8,128)(2,1)S(1)} %broadcast_in_dim.7), channel_id=1, replica_groups={{0,8,32,40,64,72,96,104,128,136,160,168,192,200,224,232,256,264,288,296..., dimensions={0} | all-to-all | bytes 1048576 | tf_op jit(solution)/shard_map/all_to_all | solution.py:317
  67.6 6.2 %collective-permute-start.1 = (bf16[32,16,512]{2,1,0:T(8,128)(2,1)S(1)}, bf16[32,16,512]{2,1,0:T(8,128)(2,1)S(1)}, u32[]{:S(2)}, u32[]{:S(2)}) collective-permute-start(bf16[32,16,512]{2,1,0:T(8,128)(2,1)S(1)} %all_to_all.32.after.own), channel_id=1, source_target_pairs={{0,16},{16,0},{1,17},{17,1},{2,18},{18,2},{3,19},{19,3},{4,20},{20... | collective-permute-start | bytes 1572872 | tf_op jit(solution)/shard_map/ppermute | solution.py:329
  73.8 0.0 copy-start
  73.8 0.0 copy-start.1
  73.8 0.3 chirp.1.a_ref
  74.2 1.2 collective-permute-done.1.other
  75.3 0.0 copy-done
  75.3 0.0 copy-done.1
  75.4 2.9 %ahead_margin.1 = (f32[8,128]{1,0:T(8,128)S(1)}, bf16[2,16,512]{2,1,0:T(8,128)(2,1)S(1)}, bf16[2,512,512]{2,1,0:T(8,128)(2,1)S(1)}, bf16[16,16,8,128]{3,2,1,0:T(8,128)(2,1)S(1)}) custom-call(s32[1]{0:T(128)} %bitcast.core_ref, s32[1]{0:T(128)} %bitcast.1.mode_ref, bf16[32,16,512]{2,1,0:T(8,128)(2,1)S(1)} %all_to_all.32.after.own, ...), custom_call_target="tpu_custom_call" | custom-call | tf_op jit(solution)/shard_map/ahead_margin/pallas_call | solution.py:226
  78.2 2.2 %collective-permute-start.2 = (bf16[16,16,8,128]{3,2,1,0:T(8,128)(2,1)S(1)}, bf16[16,16,8,128]{3,2,1,0:T(8,128)(2,1)S(1)}, u32[]{:S(2)}, u32[]{:S(2)}) collective-permute-start(bf16[16,16,8,128]{3,2,1,0:T(8,128)(2,1)S(1)} %get-tuple-element.13), channel_id=1, source_target_pairs={{0,16},{16,0},{1,17},{17,1},{2,18},{18,2},{3,19},{19,3},{4,20},{20... | collective-permute-start | bytes 1572872 | tf_op jit(solution)/shard_map/ppermute | solution.py:329
  80.5 1.0 keep_margin.1
  81.5 0.5 collective-permute-done.2
  82.0 0.1 add_convert_fusion
  82.2 13.2 %all_to_all.33 = bf16[16,16,8,128]{3,2,1,0:T(8,128)(2,1)S(1)} all-to-all(bf16[16,16,8,128]{3,2,1,0:T(8,128)(2,1)S(1)} %add_convert_fusion), channel_id=1, replica_groups={{0,32,64,96,128,160,192,224,256,288,320,352,384,416,448,480},{1,33,65,9..., dimensions={0} | all-to-all | bytes 1048576 | tf_op jit(solution)/shard_map/all_to_all | solution.py:317
  95.3 0.1 reduce_sum.47
  95.4 0.1 broadcast_in_dim.8
  95.5 17.1 %all_to_all.34.parts = bf16[16,16,8,128]{3,2,1,0:T(8,128)(2,1)S(1)} all-to-all(bf16[16,16,8,128]{3,2,1,0:T(8,128)(2,1)S(1)} %broadcast_in_dim.8), channel_id=1, replica_groups={{16,48,80,112,144,176,208,240,272,304,336,368,400,432,464,496},{17,49,8..., dimensions={0} | all-to-all | bytes 1048576 | tf_op jit(solution)/shard_map/all_to_all | solution.py:317
  112.6 0.2 tile_power.1
  112.8 11.4 %all_to_all.35.arrived = bf16[16,16,128]{2,1,0:T(8,128)(2,1)S(1)} all-to-all(bf16[16,16,128]{2,1,0:T(8,128)(2,1)S(1)} %get-tuple-element.15), channel_id=1, replica_groups={{0,32,64,96,128,160,192,224,256,288,320,352,384,416,448,480},{1,33,65,9..., dimensions={0} | all-to-all | bytes 131072 | tf_op jit(solution)/shard_map/all_to_all | solution.py:317
  124.2 6.6 %collective-permute-start.3 = (f32[8,128]{1,0:T(8,128)S(1)}, f32[8,128]{1,0:T(8,128)S(1)}, u32[]{:S(2)}, u32[]{:S(2)}) collective-permute-start(f32[8,128]{1,0:T(8,128)S(1)} %convert_reduce_fusion.power), channel_id=1, source_target_pairs={{0,16},{16,0},{1,17},{17,1},{2,18},{18,2},{3,19},{19,3},{4,20},{20... | collective-permute-start | bytes 12296 | tf_op jit(solution)/shard_map/ppermute | solution.py:329
  130.8 0.8 collective-permute-done.3.other
  131.6 0.7 tile_phasor.1
  (3 shorter events, 0.1 us)
Async XLA Ops:
  5.5 10.3 %collective-permute-start = (bf16[512,512]{1,0:T(8,128)(2,1)S(1)}, bf16[512,512]{1,0:T(8,128)(2,1)S(1)}, u32[]{:S(2)}, u32[]{:S(2)}) collective-permute-start(bf16[512,512]{1,0:T(8,128)(2,1)S(1)} %get-tuple-element.11), channel_id=1, source_target_pairs={{0,16},{16,0},{1,17},{17,1},{2,18},{18,2},{3,19},{19,3},{4,20},{20... | collective-permute-start | bytes 1572872 | tf_op jit(solution)/shard_map/ppermute | solution.py:329
  67.6 7.8 %collective-permute-start.1 = (bf16[32,16,512]{2,1,0:T(8,128)(2,1)S(1)}, bf16[32,16,512]{2,1,0:T(8,128)(2,1)S(1)}, u32[]{:S(2)}, u32[]{:S(2)}) collective-permute-start(bf16[32,16,512]{2,1,0:T(8,128)(2,1)S(1)} %all_to_all.32.after.own), channel_id=1, source_target_pairs={{0,16},{16,0},{1,17},{17,1},{2,18},{18,2},{3,19},{19,3},{4,20},{20... | collective-permute-start | bytes 1572872 | tf_op jit(solution)/shard_map/ppermute | solution.py:329
  73.8 1.5 %copy-start = (bf16[1,1,2,512,512]{4,3,2,1,0:T(8,128)(2,1)S(1)}, bf16[1,1,2,512,512]{4,3,2,1,0:T(8,128)(2,1)}, u32[]{:S(2)}) copy-start(bf16[1,1,2,512,512]{4,3,2,1,0:T(8,128)(2,1)} %param.5) | copy-start | bytes 3145732
  73.8 1.5 %copy-start.1 = (bf16[1,1,2,512,512]{4,3,2,1,0:T(8,128)(2,1)S(1)}, bf16[1,1,2,512,512]{4,3,2,1,0:T(8,128)(2,1)}, u32[]{:S(2)}) copy-start(bf16[1,1,2,512,512]{4,3,2,1,0:T(8,128)(2,1)} %param.4) | copy-start | bytes 3145732
  78.2 3.8 %collective-permute-start.2 = (bf16[16,16,8,128]{3,2,1,0:T(8,128)(2,1)S(1)}, bf16[16,16,8,128]{3,2,1,0:T(8,128)(2,1)S(1)}, u32[]{:S(2)}, u32[]{:S(2)}) collective-permute-start(bf16[16,16,8,128]{3,2,1,0:T(8,128)(2,1)S(1)} %get-tuple-element.13), channel_id=1, source_target_pairs={{0,16},{16,0},{1,17},{17,1},{2,18},{18,2},{3,19},{19,3},{4,20},{20... | collective-permute-start | bytes 1572872 | tf_op jit(solution)/shard_map/ppermute | solution.py:329
  124.2 7.4 %collective-permute-start.3 = (f32[8,128]{1,0:T(8,128)S(1)}, f32[8,128]{1,0:T(8,128)S(1)}, u32[]{:S(2)}, u32[]{:S(2)}) collective-permute-start(f32[8,128]{1,0:T(8,128)S(1)} %convert_reduce_fusion.power), channel_id=1, source_target_pairs={{0,16},{16,0},{1,17},{17,1},{2,18},{18,2},{3,19},{19,3},{4,20},{20... | collective-permute-start | bytes 12296 | tf_op jit(solution)/shard_map/ppermute | solution.py:329
